TPU v7x, 256 devices: a whole 4x4x8 slice. The times are simulated.
256 devices in a mesh: section: 4 (over x), batch: 8 (over y, core), tensor: 8 (over z).
Axes of the slice: x: 4, y: 4, z: 8, core: 2. Of those that a mesh axis runs over, the one named last changes fastest.
Arguments:
- captured: bfloat16 [4096, 3, 8192], P(('section', 'batch'), None, 'tensor'), may hold values from -6 to 6
- fc_weight: bfloat16 [3, 8192, 8192], P(None, 'tensor', ('batch', 'section')), may hold values from -0.0390625 to 0.0390625
- owner: int32 [4096, 1], replicated, may hold values from 0 to 31; in each aligned block of 128 rows (0 to 127, 128 to 255, ...) at most 12 rows name the same one
- norm_gain: float32 [8192], replicated, may hold values from 0.5 to 1.5
Outputs:
- drafted: bfloat16 [32, 8, 4, 12, 8192], P(('section', 'batch'), 'tensor')
Inputs may be any that keep to these rules, and one draw needn't show every extreme that they name: In each aligned block of 128 tokens no owner is named more than 12 times, and in some blocks one owner is named exactly 12 times; loads are skewed.
All inputs are finite; a program needn't handle non-finite values.
Results may differ from a plain program's by a relative error of at most 0.0049.
Values may be sent and summed in bfloat16 or wider, within the bound.
No kernel may reach another device: no remote copies, remote signals or barrier semaphores. Data moves between devices by JAX's collectives and lax.ppermute only.
A program may use at most 128 MiB of HBM per device.

v0:
```python
import jax
import jax.numpy as jnp
from jax import lax
from jax.sharding import PartitionSpec as P


def slot_table(block_ids, owners, slot_cap):
    onehot = (block_ids[..., None] == jnp.arange(owners, dtype=jnp.int32)).astype(jnp.int32)
    ranks = jnp.cumsum(onehot, axis=-2) - 1
    chosen = (ranks[..., None] == jnp.arange(slot_cap, dtype=jnp.int32)) & (onehot[..., None] == 1)
    return chosen.astype(jnp.bfloat16)


def body(captured, fc_weight, owner, norm_gain):
    n_section = lax.axis_size("section")
    n_batch = lax.axis_size("batch")
    n_tensor = lax.axis_size("tensor")
    owners = n_section * n_batch
    tok_dev = captured.shape[0]
    width = norm_gain.shape[0]
    class_rows = n_batch * tok_dev // n_tensor
    slot_cap = max(2, 3 * class_rows // owners)
    tensor_index = lax.axis_index("tensor")
    all_ids = owner[:, 0]
    partial_rows = jnp.einsum(
        "nlk,lkc->nc",
        lax.all_gather(captured, ("section", "batch"), axis=0, tiled=True),
        fc_weight,
        preferred_element_type=jnp.float32,
    )
    col_width = partial_rows.shape[1]
    partial_rows = partial_rows.reshape(n_section, n_batch * tok_dev, col_width)
    merged = lax.psum_scatter(partial_rows, "tensor", scatter_dimension=1, tiled=True).astype(
        jnp.bfloat16
    )
    section_ids = all_ids.reshape(n_section, n_tensor, class_rows)
    mine = lax.dynamic_index_in_dim(section_ids, tensor_index, 1, keepdims=False)
    table = slot_table(mine, owners, slot_cap)
    outgoing = jnp.einsum(
        "srom,src->osmc", table, merged, preferred_element_type=jnp.float32
    ).astype(jnp.bfloat16)
    incoming = lax.all_to_all(
        outgoing, ("section", "batch"), split_axis=0, concat_axis=0, tiled=True
    )
    incoming = incoming.reshape(n_section, n_batch, n_section, slot_cap, col_width)
    received = incoming.transpose(2, 3, 1, 0, 4).reshape(n_section, slot_cap, width)
    values = received.astype(jnp.float32)
    square_mean = jnp.mean(values * values, axis=-1, keepdims=True)
    normed = (values * lax.rsqrt(square_mean + 1e-05) * norm_gain).astype(jnp.bfloat16)
    return normed[None, None]


def solution(mesh):
    return jax.shard_map(
        body,
        mesh=mesh,
        in_specs=(
            P(("section", "batch"), None, "tensor"),
            P(None, "tensor", ("batch", "section")),
            P(),
            P(),
        ),
        out_specs=P(("section", "batch"), "tensor", None, None, None),
        check_vma=False,
    )
```

profile of v0, /device:TPU:1, one launch (start us, length us, event | category | flops | bytes accessed | tf_op | source)
XLA Modules:
  0.0 216.8 jit_solution(10564521908378880786)
XLA Ops:
  6.5 0.0 copy-start
  6.5 0.0 all-gather.2.cloned.1.call-start
  6.5 0.7 all-gather.2.cloned.1.call-update
  7.3 0.0 reduce-scatter.2.cloned.1.call-start
  7.3 104.1 %all-gather.2.cloned.1.call-done = bf16[4096,3,1024]{2,0,1:T(8,128)(2,1)} async-done(((bf16[128,3,1024]{2,0,1:T(8,128)(2,1)}), bf16[4096,3,1024]{2,0,1:T(8,128)(2,1)}) %all-gather.2.cloned.1.call-update) | async-done | bytes 25165840 | tf_op jit(solution)/shard_map/all_gather | solution.py:27
  111.4 0.0 copy-done
  111.4 13.6 %fusion.8 = f32[4096,256,1]{1,0,2:T(8,128)} fusion(bf16[4096,3,1024]{2,0,1:T(8,128)(2,1)} %all-gather.2.cloned.1.call-done, bf16[3,1024,256]{2,1,0:T(8,128)(2,1)S(1)} %copy-done), kind=kOutput, calls=%fused_computation.16 | convolution fusion | flops 6442450944 | bytes 30932992 | tf_op jit(solution)/shard_map/nlk,lkc->nc/dot_general | solution.py:25
  125.0 0.0 reduce-scatter.2.cloned.1.call-update
  125.0 0.7 constant_dynamic-slice_fusion
  125.7 0.1 broadcast_compare_fusion
  125.9 0.1 copy.15
  126.0 0.3 reduce_window_sum.11
  126.3 0.1 copy.14
  126.4 53.1 %reduce-scatter.2.cloned.1.call-done = f32[4,128,256]{2,1,0:T(8,128)} async-done(((f32[4,1024,256]{2,1,0:T(8,128)}), f32[4,128,256]{2,1,0:T(8,128)}) %reduce-scatter.2.cloned.1.call-update) | async-done | bytes 524304 | tf_op jit(solution)/shard_map/reduce_scatter | solution.py:33
  179.5 1.4 fusion
  180.9 0.6 copy.16
  181.6 21.5 %all_to_all.5 = bf16[32,4,12,256]{3,1,2,0:T(4,128)(2,1)S(1)} all-to-all(bf16[32,4,12,256]{3,1,2,0:T(4,128)(2,1)S(1)} %copy.16), channel_id=1, replica_groups=mesh['section'=4,'batch'=8,'tensor'=8] {'section','batch'}, dimensions={0} | all-to-all | bytes 1572864 | tf_op jit(solution)/shard_map/all_to_all | solution.py:42
  203.1 0.5 multiply_reduce_fusion
  203.6 0.4 convert_element_type.67
  204.0 2.2 %copy.17 = f32[4,12,8,4,256]{4,3,2,0,1:T(4,128)} copy(f32[4,12,8,4,256]{4,0,1,2,3:T(4,128)S(1)} %bitcast.19) | data formatting | bytes 3145728 | tf_op jit(solution)/shard_map/convert_element_type | solution.py:47
  206.2 0.0 copy-start.1
  206.2 2.4 %reshape.59 = f32[1,1,4,12,8192]{4,2,3,1,0:T(4,128)S(1)} reshape(f32[4,12,8,4,256]{4,3,2,0,1:T(4,128)} %copy.17) | data formatting | bytes 3145728 | tf_op jit(solution)/shard_map/convert_element_type | solution.py:47
  208.6 0.0 copy-done.1
  208.6 1.3 multiply_convert_fusion
  (2 shorter events, 0.0 us)
Async XLA Ops:
  6.5 104.9 %copy-start = (bf16[3,1024,256]{2,1,0:T(8,128)(2,1)S(1)}, bf16[3,1024,256]{2,1,0:T(8,128)(2,1)}, u32[]{:S(2)}) copy-start(bf16[3,1024,256]{2,1,0:T(8,128)(2,1)} %param.5) | copy-start | bytes 4718596
  6.5 104.9 %all-gather.2.cloned.1.call-start = ((), (), s32[]{:S(2)}) async-start(), calls=%async_computation.2 | async-start | bytes 25952256 | tf_op jit(solution)/shard_map/all_gather | solution.py:27
  7.3 172.3 %reduce-scatter.2.cloned.1.call-start = ((), (), s32[]{:S(2)}) async-start(), calls=%async_computation.3 | async-start | bytes 4718592 | tf_op jit(solution)/shard_map/reduce_scatter | solution.py:33
  206.2 2.4 %copy-start.1 = (f32[8192]{0:T(1024)S(1)}, f32[8192]{0:T(1024)}, u32[]{:S(2)}) copy-start(f32[8192]{0:T(1024)} %param.7) | copy-start | bytes 98308
Sparse Core Ops, SparseCore 0:
  10.0 101.3 all-gather.1
  125.1 54.3 reduce-scatter.1
where the time goes:
time: 217 us
  waiting for transfers between devices  158 us (73%)
  blocking collectives  21.5 us (10%)
  matrix products  15 us (7%)
  between operations  13.5 us (6%)
  local copies, waits for them, and re-layouts  6.11 us (3%)
  other arithmetic  2.72 us (1%)
    all_gather x1, waiting for transfers between devices, body(): lax.all_gather(captured, ('section', 'batch'), axis=0, tiled=True)  104 us
    reduce_scatter x1, waiting for transfers between devices, body(): lax.psum_scatter(partial_rows, 'tensor', scatter_dimension=1, tiled=True)  53.1 us
    all_to_all x1, blocking collectives, body(): lax.all_to_all(outgoing, ('section', 'batch'), split_axis=0, concat_axis=...  21.5 us
    dot_general x1, matrix products, body(): jnp.einsum('nlk,lkc->nc', lax.all_gather(captured, ('section', 'batch'),...  13.6 us
    convert_element_type x2, local copies, waits for them, and re-layouts, body(): values = received.astype(jnp.float32)  4.54 us
  transfers between devices with their start and end apart: 2, of which 2 were waited for; matrix products, arithmetic and copies ran while one was open for 1% of the time, Pallas kernels for 0%

commit v1 on v0

v1 whole, which is shorter than its diff:
```python
import jax
import jax.numpy as jnp
from jax import lax
from jax.sharding import PartitionSpec as P

SLOTS_SHARE = 3
F32 = jnp.float32
BF16 = jnp.bfloat16


def shift(value, axis, step):
    n = lax.axis_size(axis)
    return lax.ppermute(value, axis, [(i, (i + step) % n) for i in range(n)])


def hop(value, rows, cores):
    n = lax.axis_size("batch")
    pairs = [(i, ((i // 2 + rows) % (n // 2)) * 2 + (i % 2 ^ cores)) for i in range(n)]
    return lax.ppermute(value, "batch", pairs)


def slot_table(block_ids, owners, slot_cap):
    onehot = (block_ids[..., None] == jnp.arange(owners, dtype=jnp.int32)).astype(jnp.int32)
    ranks = jnp.cumsum(onehot, axis=-2) - 1
    chosen = (ranks[..., None] == jnp.arange(slot_cap, dtype=jnp.int32)) & (onehot[..., None] == 1)
    return chosen.astype(BF16)


def after(value, *earlier):
    return lax.optimization_barrier((value,) + earlier)[0]


def reduce_z(part, place, sign, earlier):
    def block(r):
        return lax.dynamic_index_in_dim(part, place(r), 0, keepdims=False)

    def pair(p, q):
        return jnp.stack([block(p).astype(BF16), block(q).astype(BF16)])

    ahead, behind, last = pair(3 * sign, sign), pair(-3 * sign, -sign), block(4).astype(BF16)
    if earlier:
        ahead, behind, last = after(ahead, *earlier), after(behind, *earlier), after(last, *earlier)
    near = shift(ahead, "tensor", sign).astype(F32)
    far = shift(last, "tensor", 2 * sign).astype(F32)
    back = shift(behind, "tensor", -sign).astype(F32)
    first = (block(2 * sign) + near[0] + far).astype(BF16)
    second = (block(-2 * sign) + back[0]).astype(BF16)
    one = shift(first, "tensor", 2 * sign)
    two = shift(second, "tensor", -2 * sign)
    total = block(0) + (near[1] + back[1]) + (one.astype(F32) + two.astype(F32))
    return total.astype(BF16), (first, second)


def body(captured, fc_weight, owner, norm_gain):
    n_section = lax.axis_size("section")
    n_batch = lax.axis_size("batch")
    n_tensor = lax.axis_size("tensor")
    owners = n_section * n_batch
    rows = captured.shape[0]
    width = norm_gain.shape[0]
    col = fc_weight.shape[2]
    slot_cap = max(2, SLOTS_SHARE * rows // owners)
    si = lax.axis_index("section")
    bi = lax.axis_index("batch")
    ti = lax.axis_index("tensor")
    yi, ci = bi // 2, bi % 2

    own = captured.transpose(1, 0, 2)
    half = col // 2
    w_up = shift(fc_weight, "section", 1)
    w_dn = shift(fc_weight, "section", -1)
    y_up = hop(own, 1, 0)
    y_dn = hop(own, -1, 0)
    sib = hop(own, 0, 1)
    r2 = rows // 2
    far_top = hop(y_up[:, :r2], 1, 0)
    far_bot = hop(y_dn[:, r2:], -1, 0)
    y_up_s = hop(y_up, 0, 1)
    y_dn_s = hop(y_dn, 0, 1)
    far_a = shift(w_up[:, :, :half], "section", 1)
    far_b = shift(w_dn[:, :, half:], "section", -1)
    y_far = jnp.concatenate([far_top, far_bot], axis=1)
    y_far_s = hop(y_far, 0, 1)
    tokens = jnp.concatenate(
        [own, sib, y_dn, y_dn_s, y_far, y_far_s, y_up, y_up_s], axis=1
    )

    def place(r):
        target = (ti + r) % n_tensor
        return ((target // 2 - yi) % (n_batch // 2)) * 2 + (target % 2 ^ ci)

    mine = lax.dynamic_index_in_dim(
        owner[:, 0].reshape(n_section * n_tensor, rows), si * n_tensor + ti, 0, keepdims=False
    )
    table = slot_table(mine, owners, slot_cap)

    def job(weights, sign, earlier):
        weight = jnp.concatenate(weights, axis=2)
        part = jnp.einsum("lnk,lkc->nc", tokens, weight, preferred_element_type=F32)
        part = part.reshape(n_batch, rows, weight.shape[2])
        return reduce_z(part, place, sign, earlier)

    first, _ = job([fc_weight, w_up, w_dn], 1, ())
    second, _ = job([far_a, far_b], -1, ())
    done = [first, second]
    merged = jnp.concatenate(done, axis=1)
    outgoing = jnp.einsum("rom,rc->omc", table, merged, preferred_element_type=F32).astype(BF16)
    incoming = lax.all_to_all(
        outgoing, ("section", "batch"), split_axis=0, concat_axis=0, tiled=True
    )
    incoming = incoming.reshape(n_section, n_batch, slot_cap, n_section, col)
    rows_of = []
    for s in range(n_section):
        order = {(s + d) % n_section: i for i, d in enumerate((0, -1, 1, 2))}
        parts = [incoming[s, :, :, order[p]] for p in range(n_section)]
        rows_of.append(jnp.stack(parts, axis=2).transpose(1, 0, 2, 3).reshape(slot_cap, width))
    values = jnp.stack(rows_of, axis=1).astype(F32)
    square_mean = jnp.mean(values * values, axis=-1, keepdims=True)
    normed = (values * lax.rsqrt(square_mean + 1e-05) * norm_gain).astype(BF16)
    return normed.transpose(1, 0, 2)[None, None]


def solution(mesh):
    return jax.shard_map(
        body,
        mesh=mesh,
        in_specs=(
            P(("section", "batch"), None, "tensor"),
            P(None, "tensor", ("batch", "section")),
            P(),
            P(),
        ),
        out_specs=P(("section", "batch"), "tensor", None, None, None),
        check_vma=False,
    )
```

time: 217 us -> 127 us (0.59)
  waiting for transfers between devices: 158 us -> 30.5 us
  starting transfers between devices: 0.04 us -> 40.2 us
  between operations: 13.5 us -> 0.54 us
  blocking collectives: 21.5 us -> 29 us
  local copies, waits for them, and re-layouts: 6.11 us -> 13.2 us
  matrix products: 15 us -> 9.05 us
    all_gather x1 -> x0, waiting for transfers between devices: 104 us -> none  [body(): lax.all_gather(captured, ('section', 'batch'), axis=0, tiled=True)]
    reduce_scatter x1 -> x0, waiting for transfers between devices: 53.1 us -> none  [body(): lax.psum_scatter(partial_rows, 'tensor', scatter_dimension=1, tiled=True)]
    ppermute x0 -> x22, starting transfers between devices: none -> 40.2 us  [the longest x14 26.2 us: shift(): return lax.ppermute(value, axis, [(i, (i + step) % n) for i in range(n)])]
    ppermute x0 -> x22, waiting for transfers between devices: none -> 30.5 us  [the longest x14 17 us: shift(): return lax.ppermute(value, axis, [(i, (i + step) % n) for i in range(n)])]
    all_to_all x1, blocking collectives: 21.5 us -> 29 us  [body(): lax.all_to_all(outgoing, ('section', 'batch'), split_axis=0, concat_axis=...]
    dot_general x2 -> x3, matrix products: 15 us -> 9.05 us  [the longest x2 8.7 us: job(): part = jnp.einsum('lnk,lkc->nc', tokens, weight, preferred_element_type=F32)]
    slice x0 -> x5, local copies, waits for them, and re-layouts: none -> 4.75 us  [the longest x1 1.58 us: body(): parts = [incoming[s, :, :, order[p]] for p in range(n_section)]]
    convert_element_type x3, local copies, waits for them, and re-layouts: 5.16 us -> 0.6 us  [the longest x1 0.45 us: body(): jnp.einsum('rom,rc->omc', table, merged, preferred_element_type=F32)]
  transfers between devices with their start and end apart: 2 -> 22, of which waited for: 2 -> 8; matrix products, arithmetic and copies ran while one was open for 1% -> 16% of each run, Pallas kernels for 0% -> 0%
where the time goes in v1:
time: 127 us
  starting transfers between devices  40.2 us (32%)
  waiting for transfers between devices  30.5 us (24%)
  blocking collectives  29 us (23%)
  local copies, waits for them, and re-layouts  13.2 us (10%)
  matrix products  9.05 us (7%)
  other arithmetic  4.54 us (4%)
    all_to_all x1, blocking collectives, body(): lax.all_to_all(outgoing, ('section', 'batch'), split_axis=0, concat_axis=...  29 us
    ppermute x14, starting transfers between devices, shift(): return lax.ppermute(value, axis, [(i, (i + step) % n) for i in range(n)])  26.2 us
    ppermute x14, waiting for transfers between devices, shift(): return lax.ppermute(value, axis, [(i, (i + step) % n) for i in range(n)])  17 us
    ppermute x8, starting transfers between devices, hop(): return lax.ppermute(value, 'batch', pairs)  14 us
    ppermute x8, waiting for transfers between devices, hop(): return lax.ppermute(value, 'batch', pairs)  13.6 us
    dot_general x2, matrix products, job(): part = jnp.einsum('lnk,lkc->nc', tokens, weight, preferred_element_type=F32)  8.7 us
    unnamed x26, local copies, waits for them, and re-layouts  2.96 us
  transfers between devices with their start and end apart: 22, of which 8 were waited for; matrix products, arithmetic and copies ran while one was open for 16% of the time, Pallas kernels for 0%

profile of v1, /device:TPU:1, one launch (start us, length us, event | category | flops | bytes accessed | tf_op | source)
XLA Modules:
  0.0 127.0 jit_solution(14854417121127220513)
XLA Ops:
  0.0 2.1 %collective-permute-start.3 = (bf16[3,128,1024]{2,1,0:T(8,128)(2,1)}, bf16[3,128,1024]{2,1,0:T(8,128)(2,1)S(1)}, u32[]{:S(2)}, u32[]{:S(2)}) collective-permute-start(bf16[3,128,1024]{2,1,0:T(8,128)(2,1)} %bitcast.113), channel_id=1, source_target_pairs={{0,16},{8,24},{16,32},{24,40},{32,48},{40,56},{48,0},{56,8},{1,17}... | collective-permute-start | bytes 2359304 | tf_op jit(solution)/shard_map/ppermute | solution.py:19
  2.1 1.5 %collective-permute-start.1 = (bf16[3,128,1024]{2,1,0:T(8,128)(2,1)}, bf16[3,128,1024]{2,1,0:T(8,128)(2,1)S(1)}, u32[]{:S(2)}, u32[]{:S(2)}) collective-permute-start(bf16[3,128,1024]{2,1,0:T(8,128)(2,1)} %bitcast.114), channel_id=1, source_target_pairs={{0,48},{8,56},{16,0},{24,8},{32,16},{40,24},{48,32},{56,40},{1,49}... | collective-permute-start | bytes 2359304 | tf_op jit(solution)/shard_map/ppermute | solution.py:19
  3.7 2.5 %collective-permute-start.9 = (bf16[3,1024,256]{2,1,0:T(8,128)(2,1)}, bf16[3,1024,256]{2,1,0:T(8,128)(2,1)}, u32[]{:S(2)}, u32[]{:S(2)}) collective-permute-start(bf16[3,1024,256]{2,1,0:T(8,128)(2,1)} %param.5), channel_id=1, source_target_pairs={{0,192},{64,0},{128,64},{192,128},{1,193},{65,1},{129,65},{193,129... | collective-permute-start | bytes 4718600 | tf_op jit(solution)/shard_map/ppermute | solution.py:13
  6.1 13.0 %collective-permute-done.3 = bf16[3,128,1024]{2,1,0:T(8,128)(2,1)S(1)} collective-permute-done((bf16[3,128,1024]{2,1,0:T(8,128)(2,1)}, bf16[3,128,1024]{2,1,0:T(8,128)(2,1)S(1)}, u32[]{:S(2)}, u32[]{:S(2)}) %collective-permute-start.3) | collective-permute-done | bytes 786464 | tf_op jit(solution)/shard_map/ppermute | solution.py:19
  19.1 1.6 %collective-permute-start.4 = (bf16[3,64,1024]{2,1,0:T(8,128)(2,1)S(1)}, bf16[3,64,1024]{2,1,0:T(8,128)(2,1)S(1)}, u32[]{:S(2)}, u32[]{:S(2)}) collective-permute-start(bf16[3,64,1024]{2,1,0:T(8,128)(2,1)S(1)} %slice.112), channel_id=1, source_target_pairs={{0,16},{8,24},{16,32},{24,40},{32,48},{40,56},{48,0},{56,8},{1,17}... | collective-permute-start | bytes 1179656 | tf_op jit(solution)/shard_map/ppermute | solution.py:19
  20.8 1.9 %collective-permute-start = (bf16[3,128,1024]{2,1,0:T(8,128)(2,1)}, bf16[3,128,1024]{2,1,0:T(8,128)(2,1)S(1)}, u32[]{:S(2)}, u32[]{:S(2)}) collective-permute-start(bf16[3,128,1024]{2,1,0:T(8,128)(2,1)} %bitcast.115), channel_id=1, source_target_pairs={{0,8},{8,0},{16,24},{24,16},{32,40},{40,32},{48,56},{56,48},{1,9},... | collective-permute-start | bytes 2359304 | tf_op jit(solution)/shard_map/ppermute | solution.py:19
  22.7 0.8 slice.113
  23.5 2.7 %collective-permute-start.5 = (bf16[3,64,1024]{2,1,0:T(8,128)(2,1)}, bf16[3,64,1024]{2,1,0:T(8,128)(2,1)S(1)}, u32[]{:S(2)}, u32[]{:S(2)}) collective-permute-start(bf16[3,64,1024]{2,1,0:T(8,128)(2,1)} %slice.113), channel_id=1, source_target_pairs={{0,48},{8,56},{16,0},{24,8},{32,16},{40,24},{48,32},{56,40},{1,49}... | collective-permute-start | bytes 1179656 | tf_op jit(solution)/shard_map/ppermute | solution.py:19
  26.1 0.7 broadcast_compare_fusion
  26.8 1.6 %reduce_window_sum.11 = s32[128,32]{1,0:T(8,128)} reduce-window(s32[128,32]{1,0:T(8,128)} %get-tuple-element.32, s32[]{:T(128)} %constant.312.clone.1), window={size=128x1 pad=127_0x0_0}, to_apply=%region_0.1 | reduce-window | flops 520192 | bytes 32772 | tf_op jit(solution)/shard_map/jit(cumsum)/reduce_window_sum | solution.py:24
  28.4 0.6 collective-permute-done.4
  29.0 3.5 %collective-permute-start.2 = (bf16[3,128,1024]{2,1,0:T(8,128)(2,1)S(1)}, bf16[3,128,1024]{2,1,0:T(8,128)(2,1)}, u32[]{:S(2)}, u32[]{:S(2)}) collective-permute-start(bf16[3,128,1024]{2,1,0:T(8,128)(2,1)S(1)} %collective-permute-done.1), channel_id=1, source_target_pairs={{0,8},{8,0},{16,24},{24,16},{32,40},{40,32},{48,56},{56,48},{1,9},... | collective-permute-start | bytes 2359304 | tf_op jit(solution)/shard_map/ppermute | solution.py:19
  32.5 0.8 broadcast_add_fusion
  33.3 0.7 copy.73
  34.0 1.4 %copy.74 = pred[128,32]{0,1:T(8,128)(4,1)} copy(pred[128,32]{1,0:T(8,128)(4,1)} %get-tuple-element.31) | data formatting | bytes 8192 | tf_op jit(solution)/shard_map/eq | solution.py:25
  35.4 0.5 collective-permute-start.6
  35.9 1.2 constant_dynamic-update-slice_fusion.8
  37.1 0.2 collective-permute-start.7
  37.4 1.6 %collective-permute-done.9 = bf16[3,1024,256]{2,1,0:T(8,128)(2,1)} collective-permute-done((bf16[3,1024,256]{2,1,0:T(8,128)(2,1)}, bf16[3,1024,256]{2,1,0:T(8,128)(2,1)}, u32[]{:S(2)}, u32[]{:S(2)}) %collective-permute-start.9) | collective-permute-done | bytes 1572896 | tf_op jit(solution)/shard_map/ppermute | solution.py:13
  39.0 1.2 slice.119
  40.2 3.5 %collective-permute-start.16 = (bf16[3,1024,128]{2,1,0:T(8,128)(2,1)S(1)}, bf16[3,1024,128]{2,1,0:T(8,128)(2,1)S(1)}, u32[]{:S(2)}, u32[]{:S(2)}) collective-permute-start(bf16[3,1024,128]{2,1,0:T(8,128)(2,1)S(1)} %slice.119), channel_id=1, source_target_pairs={{0,192},{64,0},{128,64},{192,128},{1,193},{65,1},{129,65},{193,129... | collective-permute-start | bytes 2359304 | tf_op jit(solution)/shard_map/ppermute | solution.py:13
  43.7 1.2 slice.118
  44.9 0.3 collective-permute-start.15
  45.2 1.2 constant_dynamic-update-slice_fusion.5
  46.7 6.9 %fusion = f32[1024,768,1]{1,0,2:T(8,128)S(1)} fusion(bf16[3,1024,1024]{2,1,0:T(8,128)(2,1)S(1)} %constant_dynamic-update-slice_fusion, bf16[3,1024,256]{2,1,0:T(8,128)(2,1)} %collective-permute-done.9, bf16[3,1024,256]{2,1,0:T(8,128)(2,1)} %collective-permute-done.8, bf16[3,1024,256]{2,1,0:T(8,128)(2,1)S(1)} %copy-done.4), kind=kOutput, calls=%fused_computation | convolution fusion | flops 4845993984 | bytes 14155776 | tf_op jit(solution)/shard_map/lnk,lkc->nc/dot_general | solution.py:99
  53.7 5.7 %collective-permute-start.11 = (bf16[2,128,768]{2,1,0:T(8,128)(2,1)S(1)}, bf16[2,128,768]{2,1,0:T(8,128)(2,1)S(1)}, u32[]{:S(2)}, u32[]{:S(2)}) collective-permute-start(bf16[2,128,768]{2,1,0:T(8,128)(2,1)S(1)} %pad_maximum_fusion.3), channel_id=1, source_target_pairs={{0,7},{1,0},{2,1},{3,2},{4,3},{5,4},{6,5},{7,6},{8,15},{9,8},{10,9... | collective-permute-start | bytes 1179656 | tf_op jit(solution)/shard_map/ppermute | solution.py:13
  59.6 3.5 %collective-permute-done.15 = bf16[3,1024,128]{2,1,0:T(8,128)(2,1)S(1)} collective-permute-done((bf16[3,1024,128]{2,1,0:T(8,128)(2,1)S(1)}, bf16[3,1024,128]{2,1,0:T(8,128)(2,1)S(1)}, u32[]{:S(2)}, u32[]{:S(2)}) %collective-permute-start.15) | collective-permute-done | bytes 786464 | tf_op jit(solution)/shard_map/ppermute | solution.py:13
  63.1 1.8 %fusion.9 = f32[1024,256,1]{1,0,2:T(8,128)S(1)} fusion(bf16[3,1024,1024]{2,1,0:T(8,128)(2,1)S(1)} %constant_dynamic-update-slice_fusion, bf16[3,1024,128]{2,1,0:T(8,128)(2,1)S(1)} %collective-permute-done.16, bf16[3,1024,128]{2,1,0:T(8,128)(2,1)S(1)} %collective-permute-done.15), kind=kOutput, calls=%fused_computation.11 | convolution fusion | flops 1613758464 | bytes 8912896 | tf_op jit(solution)/shard_map/lnk,lkc->nc/dot_general | solution.py:99
  65.0 1.7 %collective-permute-start.18 = (bf16[2,128,256]{2,1,0:T(8,128)(2,1)S(1)}, bf16[2,128,256]{2,1,0:T(8,128)(2,1)S(1)}, u32[]{:S(2)}, u32[]{:S(2)}) collective-permute-start(bf16[2,128,256]{2,1,0:T(8,128)(2,1)S(1)} %pad_maximum_fusion.5), channel_id=1, source_target_pairs={{0,1},{1,2},{2,3},{3,4},{4,5},{5,6},{6,7},{7,0},{8,9},{9,10},{10,1... | collective-permute-start | bytes 393224 | tf_op jit(solution)/shard_map/ppermute | solution.py:13
  66.7 4.0 %collective-permute-start.17 = (bf16[2,128,256]{2,1,0:T(8,128)(2,1)S(1)}, bf16[2,128,256]{2,1,0:T(8,128)(2,1)S(1)}, u32[]{:S(2)}, u32[]{:S(2)}) collective-permute-start(bf16[2,128,256]{2,1,0:T(8,128)(2,1)S(1)} %pad_maximum_fusion.4), channel_id=1, source_target_pairs={{0,7},{1,0},{2,1},{3,2},{4,3},{5,4},{6,5},{7,6},{8,15},{9,8},{10,9... | collective-permute-start | bytes 393224 | tf_op jit(solution)/shard_map/ppermute | solution.py:13
  70.8 1.9 %collective-permute-start.19 = (bf16[128,256]{1,0:T(8,128)(2,1)S(1)}, bf16[128,256]{1,0:T(8,128)(2,1)S(1)}, u32[]{:S(2)}, u32[]{:S(2)}) collective-permute-start(bf16[128,256]{1,0:T(8,128)(2,1)S(1)} %get-tuple-element.10), channel_id=1, source_target_pairs={{0,6},{1,7},{2,0},{3,1},{4,2},{5,3},{6,4},{7,5},{8,14},{9,15},{10,... | collective-permute-start | bytes 196616 | tf_op jit(solution)/shard_map/ppermute | solution.py:13
  72.8 2.5 %collective-permute-start.14 = (bf16[128,768]{1,0:T(8,128)(2,1)S(1)}, bf16[128,768]{1,0:T(8,128)(2,1)S(1)}, u32[]{:S(2)}, u32[]{:S(2)}) collective-permute-start(bf16[128,768]{1,0:T(8,128)(2,1)S(1)} %fusion.25), channel_id=1, source_target_pairs={{0,6},{1,7},{2,0},{3,1},{4,2},{5,3},{6,4},{7,5},{8,14},{9,15},{10,... | collective-permute-start | bytes 589832 | tf_op jit(solution)/shard_map/ppermute | solution.py:13
  75.3 4.5 %collective-permute-done.18 = bf16[2,128,256]{2,1,0:T(8,128)(2,1)S(1)} collective-permute-done((bf16[2,128,256]{2,1,0:T(8,128)(2,1)S(1)}, bf16[2,128,256]{2,1,0:T(8,128)(2,1)S(1)}, u32[]{:S(2)}, u32[]{:S(2)}) %collective-permute-start.18) | collective-permute-done | bytes 131104 | tf_op jit(solution)/shard_map/ppermute | solution.py:13
  80.1 3.8 %collective-permute-start.20 = (bf16[128,256]{1,0:T(8,128)(2,1)S(1)}, bf16[128,256]{1,0:T(8,128)(2,1)S(1)}, u32[]{:S(2)}, u32[]{:S(2)}) collective-permute-start(bf16[128,256]{1,0:T(8,128)(2,1)S(1)} %fusion.31), channel_id=1, source_target_pairs={{0,6},{1,7},{2,0},{3,1},{4,2},{5,3},{6,4},{7,5},{8,14},{9,15},{10,... | collective-permute-start | bytes 196616 | tf_op jit(solution)/shard_map/ppermute | solution.py:13
  84.1 3.4 %collective-permute-done.21 = bf16[128,256]{1,0:T(8,128)(2,1)S(1)} collective-permute-done((bf16[128,256]{1,0:T(8,128)(2,1)S(1)}, bf16[128,256]{1,0:T(8,128)(2,1)S(1)}, u32[]{:S(2)}, u32[]{:S(2)}) %collective-permute-start.21) | collective-permute-done | bytes 65568 | tf_op jit(solution)/shard_map/ppermute | solution.py:13
  87.4 0.2 collective-permute-done.20
  87.7 3.7 %collective-permute-done.13 = bf16[128,768]{1,0:T(8,128)(2,1)S(1)} collective-permute-done((bf16[128,768]{1,0:T(8,128)(2,1)S(1)}, bf16[128,768]{1,0:T(8,128)(2,1)S(1)}, u32[]{:S(2)}, u32[]{:S(2)}) %collective-permute-start.13) | collective-permute-done | bytes 196640 | tf_op jit(solution)/shard_map/ppermute | solution.py:13
  91.6 0.4 convolution_convert_fusion
  92.0 0.4 copy.75
  92.4 29.0 %all_to_all.5 = bf16[32,12,1024]{2,1,0:T(8,128)(2,1)S(1)} all-to-all(bf16[32,12,1024]{2,1,0:T(8,128)(2,1)S(1)} %copy.75), channel_id=1, replica_groups=mesh['section'=4,'batch'=8,'tensor'=8] {'section','batch'}, dimensions={0} | all-to-all | bytes 1572864 | tf_op jit(solution)/shard_map/all_to_all | solution.py:108
  121.4 0.4 reshape.92
  121.9 1.6 %fusion.45 = (bf16[1,8,12,1,256]{4,3,2,1,0:T(2,128)(2,1)S(1)}, bf16[1,8,12,1,256]{4,3,2,1,0:T(2,128)(2,1)S(1)}, bf16[1,8,12,1,256]{4,3,2,1,0:T(2,128)(2,1)S(1)},...) fusion(bf16[4,8,12,4,256]{4,3,2,1,0:T(4,128)(2,1)S(1)} %reshape.92), kind=kLoop, calls=%fused_computation.105 | loop fusion | bytes 1572864 | tf_op jit(solution)/shard_map/slice | solution.py:115
  123.7 0.1 stack_reshape.15
  124.0 0.1 stack_reshape.14
  124.3 0.1 stack_reshape.13
  124.8 0.4 fusion.6
  125.2 0.3 fusion.13
  125.5 1.5 %copy.81 = bf16[1,1,4,12,8192]{4,2,3,1,0:T(4,128)(2,1)} copy(bf16[1,1,4,12,8192]{4,3,2,1,0:T(8,128)(2,1)S(1)} %fusion.13) | data formatting | bytes 1572864 | tf_op jit(solution)/shard_map/broadcast_in_dim | solution.py:120
  (73 shorter events, 2.4 us)
Async XLA Ops:
  0.0 22.7 %copy-start = (s32[4096,1]{0,1:T(1,128)S(1)}, s32[4096,1]{0,1:T(1,128)}, u32[]{:S(2)}) copy-start(s32[4096,1]{0,1:T(1,128)} %param.6) | copy-start | bytes 49156
  0.0 19.1 %collective-permute-start.3 = (bf16[3,128,1024]{2,1,0:T(8,128)(2,1)}, bf16[3,128,1024]{2,1,0:T(8,128)(2,1)S(1)}, u32[]{:S(2)}, u32[]{:S(2)}) collective-permute-start(bf16[3,128,1024]{2,1,0:T(8,128)(2,1)} %bitcast.113), channel_id=1, source_target_pairs={{0,16},{8,24},{16,32},{24,40},{32,48},{40,56},{48,0},{56,8},{1,17}... | collective-permute-start | bytes 2359304 | tf_op jit(solution)/shard_map/ppermute | solution.py:19
  2.1 20.6 %collective-permute-start.1 = (bf16[3,128,1024]{2,1,0:T(8,128)(2,1)}, bf16[3,128,1024]{2,1,0:T(8,128)(2,1)S(1)}, u32[]{:S(2)}, u32[]{:S(2)}) collective-permute-start(bf16[3,128,1024]{2,1,0:T(8,128)(2,1)} %bitcast.114), channel_id=1, source_target_pairs={{0,48},{8,56},{16,0},{24,8},{32,16},{40,24},{48,32},{56,40},{1,49}... | collective-permute-start | bytes 2359304 | tf_op jit(solution)/shard_map/ppermute | solution.py:19
  3.7 35.4 %collective-permute-start.9 = (bf16[3,1024,256]{2,1,0:T(8,128)(2,1)}, bf16[3,1024,256]{2,1,0:T(8,128)(2,1)}, u32[]{:S(2)}, u32[]{:S(2)}) collective-permute-start(bf16[3,1024,256]{2,1,0:T(8,128)(2,1)} %param.5), channel_id=1, source_target_pairs={{0,192},{64,0},{128,64},{192,128},{1,193},{65,1},{129,65},{193,129... | collective-permute-start | bytes 4718600 | tf_op jit(solution)/shard_map/ppermute | solution.py:13
  6.1 37.6 %collective-permute-start.8 = (bf16[3,1024,256]{2,1,0:T(8,128)(2,1)}, bf16[3,1024,256]{2,1,0:T(8,128)(2,1)}, u32[]{:S(2)}, u32[]{:S(2)}) collective-permute-start(bf16[3,1024,256]{2,1,0:T(8,128)(2,1)} %param.5), channel_id=1, source_target_pairs={{0,64},{64,128},{128,192},{192,0},{1,65},{65,129},{129,193},{193,1... | collective-permute-start | bytes 4718600 | tf_op jit(solution)/shard_map/ppermute | solution.py:13
  19.1 9.9 %collective-permute-start.4 = (bf16[3,64,1024]{2,1,0:T(8,128)(2,1)S(1)}, bf16[3,64,1024]{2,1,0:T(8,128)(2,1)S(1)}, u32[]{:S(2)}, u32[]{:S(2)}) collective-permute-start(bf16[3,64,1024]{2,1,0:T(8,128)(2,1)S(1)} %slice.112), channel_id=1, source_target_pairs={{0,16},{8,24},{16,32},{24,40},{32,48},{40,56},{48,0},{56,8},{1,17}... | collective-permute-start | bytes 1179656 | tf_op jit(solution)/shard_map/ppermute | solution.py:19
  20.8 16.3 %collective-permute-start = (bf16[3,128,1024]{2,1,0:T(8,128)(2,1)}, bf16[3,128,1024]{2,1,0:T(8,128)(2,1)S(1)}, u32[]{:S(2)}, u32[]{:S(2)}) collective-permute-start(bf16[3,128,1024]{2,1,0:T(8,128)(2,1)} %bitcast.115), channel_id=1, source_target_pairs={{0,8},{8,0},{16,24},{24,16},{32,40},{40,32},{48,56},{56,48},{1,9},... | collective-permute-start | bytes 2359304 | tf_op jit(solution)/shard_map/ppermute | solution.py:19
  23.5 11.9 %collective-permute-start.5 = (bf16[3,64,1024]{2,1,0:T(8,128)(2,1)}, bf16[3,64,1024]{2,1,0:T(8,128)(2,1)S(1)}, u32[]{:S(2)}, u32[]{:S(2)}) collective-permute-start(bf16[3,64,1024]{2,1,0:T(8,128)(2,1)} %slice.113), channel_id=1, source_target_pairs={{0,48},{8,56},{16,0},{24,8},{32,16},{40,24},{48,32},{56,40},{1,49}... | collective-permute-start | bytes 1179656 | tf_op jit(solution)/shard_map/ppermute | solution.py:19
  29.0 16.2 %collective-permute-start.2 = (bf16[3,128,1024]{2,1,0:T(8,128)(2,1)S(1)}, bf16[3,128,1024]{2,1,0:T(8,128)(2,1)}, u32[]{:S(2)}, u32[]{:S(2)}) collective-permute-start(bf16[3,128,1024]{2,1,0:T(8,128)(2,1)S(1)} %collective-permute-done.1), channel_id=1, source_target_pairs={{0,8},{8,0},{16,24},{24,16},{32,40},{40,32},{48,56},{56,48},{1,9},... | collective-permute-start | bytes 2359304 | tf_op jit(solution)/shard_map/ppermute | solution.py:19
  35.4 11.0 %collective-permute-start.6 = (bf16[3,128,1024]{2,1,0:T(8,128)(2,1)S(1)}, bf16[3,128,1024]{2,1,0:T(8,128)(2,1)S(1)}, u32[]{:S(2)}, u32[]{:S(2)}) collective-permute-start(bf16[3,128,1024]{2,1,0:T(8,128)(2,1)S(1)} %pad_maximum_fusion.1), channel_id=1, source_target_pairs={{0,8},{8,0},{16,24},{24,16},{32,40},{40,32},{48,56},{56,48},{1,9},... | collective-permute-start | bytes 2359304 | tf_op jit(solution)/shard_map/ppermute | solution.py:19
  37.1 9.5 %collective-permute-start.7 = (bf16[3,128,1024]{2,1,0:T(8,128)(2,1)S(1)}, bf16[3,128,1024]{2,1,0:T(8,128)(2,1)S(1)}, u32[]{:S(2)}, u32[]{:S(2)}) collective-permute-start(bf16[3,128,1024]{2,1,0:T(8,128)(2,1)S(1)} %collective-permute-done.3), channel_id=1, source_target_pairs={{0,8},{8,0},{16,24},{24,16},{32,40},{40,32},{48,56},{56,48},{1,9},... | collective-permute-start | bytes 2359304 | tf_op jit(solution)/shard_map/ppermute | solution.py:19
  37.4 9.3 %copy-start.4 = (bf16[3,1024,256]{2,1,0:T(8,128)(2,1)S(1)}, bf16[3,1024,256]{2,1,0:T(8,128)(2,1)}, u32[]{:S(2)}) copy-start(bf16[3,1024,256]{2,1,0:T(8,128)(2,1)} %param.5) | copy-start | bytes 4718596
  40.2 19.4 %collective-permute-start.16 = (bf16[3,1024,128]{2,1,0:T(8,128)(2,1)S(1)}, bf16[3,1024,128]{2,1,0:T(8,128)(2,1)S(1)}, u32[]{:S(2)}, u32[]{:S(2)}) collective-permute-start(bf16[3,1024,128]{2,1,0:T(8,128)(2,1)S(1)} %slice.119), channel_id=1, source_target_pairs={{0,192},{64,0},{128,64},{192,128},{1,193},{65,1},{129,65},{193,129... | collective-permute-start | bytes 2359304 | tf_op jit(solution)/shard_map/ppermute | solution.py:13
  44.9 18.2 %collective-permute-start.15 = (bf16[3,1024,128]{2,1,0:T(8,128)(2,1)S(1)}, bf16[3,1024,128]{2,1,0:T(8,128)(2,1)S(1)}, u32[]{:S(2)}, u32[]{:S(2)}) collective-permute-start(bf16[3,1024,128]{2,1,0:T(8,128)(2,1)S(1)} %slice.118), channel_id=1, source_target_pairs={{0,64},{64,128},{128,192},{192,0},{1,65},{65,129},{129,193},{193,1... | collective-permute-start | bytes 2359304 | tf_op jit(solution)/shard_map/ppermute | solution.py:13
  53.7 17.0 %collective-permute-start.11 = (bf16[2,128,768]{2,1,0:T(8,128)(2,1)S(1)}, bf16[2,128,768]{2,1,0:T(8,128)(2,1)S(1)}, u32[]{:S(2)}, u32[]{:S(2)}) collective-permute-start(bf16[2,128,768]{2,1,0:T(8,128)(2,1)S(1)} %pad_maximum_fusion.3), channel_id=1, source_target_pairs={{0,7},{1,0},{2,1},{3,2},{4,3},{5,4},{6,5},{7,6},{8,15},{9,8},{10,9... | collective-permute-start | bytes 1179656 | tf_op jit(solution)/shard_map/ppermute | solution.py:13
  59.4 13.3 %collective-permute-start.10 = (bf16[2,128,768]{2,1,0:T(8,128)(2,1)S(1)}, bf16[2,128,768]{2,1,0:T(8,128)(2,1)S(1)}, u32[]{:S(2)}, u32[]{:S(2)}) collective-permute-start(bf16[2,128,768]{2,1,0:T(8,128)(2,1)S(1)} %pad_maximum_fusion.2), channel_id=1, source_target_pairs={{0,1},{1,2},{2,3},{3,4},{4,5},{5,6},{6,7},{7,0},{8,9},{9,10},{10,1... | collective-permute-start | bytes 1179656 | tf_op jit(solution)/shard_map/ppermute | solution.py:13
  59.5 24.4 %collective-permute-start.12 = (bf16[128,768]{1,0:T(8,128)(2,1)S(1)}, bf16[128,768]{1,0:T(8,128)(2,1)S(1)}, u32[]{:S(2)}, u32[]{:S(2)}) collective-permute-start(bf16[128,768]{1,0:T(8,128)(2,1)S(1)} %get-tuple-element.5), channel_id=1, source_target_pairs={{0,2},{1,3},{2,4},{3,5},{4,6},{5,7},{6,0},{7,1},{8,10},{9,11},{10,... | collective-permute-start | bytes 589832 | tf_op jit(solution)/shard_map/ppermute | solution.py:13
  64.9 26.7 %copy-start.1 = (s32[128,32]{0,1:T(8,128)S(1)}, s32[128,32]{0,1:T(8,128)}, u32[]{:S(2)}) copy-start(s32[128,32]{0,1:T(8,128)} %copy.73) | copy-start | bytes 49156
  64.9 26.7 %copy-start.3 = (pred[128,32]{0,1:T(8,128)(4,1)S(1)}, pred[128,32]{0,1:T(8,128)(4,1)}, u32[]{:S(2)}) copy-start(pred[128,32]{0,1:T(8,128)(4,1)} %copy.74) | copy-start | bytes 12292
  65.0 14.8 %collective-permute-start.18 = (bf16[2,128,256]{2,1,0:T(8,128)(2,1)S(1)}, bf16[2,128,256]{2,1,0:T(8,128)(2,1)S(1)}, u32[]{:S(2)}, u32[]{:S(2)}) collective-permute-start(bf16[2,128,256]{2,1,0:T(8,128)(2,1)S(1)} %pad_maximum_fusion.5), channel_id=1, source_target_pairs={{0,1},{1,2},{2,3},{3,4},{4,5},{5,6},{6,7},{7,0},{8,9},{9,10},{10,1... | collective-permute-start | bytes 393224 | tf_op jit(solution)/shard_map/ppermute | solution.py:13
  66.7 13.2 %collective-permute-start.17 = (bf16[2,128,256]{2,1,0:T(8,128)(2,1)S(1)}, bf16[2,128,256]{2,1,0:T(8,128)(2,1)S(1)}, u32[]{:S(2)}, u32[]{:S(2)}) collective-permute-start(bf16[2,128,256]{2,1,0:T(8,128)(2,1)S(1)} %pad_maximum_fusion.4), channel_id=1, source_target_pairs={{0,7},{1,0},{2,1},{3,2},{4,3},{5,4},{6,5},{7,6},{8,15},{9,8},{10,9... | collective-permute-start | bytes 393224 | tf_op jit(solution)/shard_map/ppermute | solution.py:13
  70.8 9.2 %collective-permute-start.19 = (bf16[128,256]{1,0:T(8,128)(2,1)S(1)}, bf16[128,256]{1,0:T(8,128)(2,1)S(1)}, u32[]{:S(2)}, u32[]{:S(2)}) collective-permute-start(bf16[128,256]{1,0:T(8,128)(2,1)S(1)} %get-tuple-element.10), channel_id=1, source_target_pairs={{0,6},{1,7},{2,0},{3,1},{4,2},{5,3},{6,4},{7,5},{8,14},{9,15},{10,... | collective-permute-start | bytes 196616 | tf_op jit(solution)/shard_map/ppermute | solution.py:13
  72.8 14.9 %collective-permute-start.14 = (bf16[128,768]{1,0:T(8,128)(2,1)S(1)}, bf16[128,768]{1,0:T(8,128)(2,1)S(1)}, u32[]{:S(2)}, u32[]{:S(2)}) collective-permute-start(bf16[128,768]{1,0:T(8,128)(2,1)S(1)} %fusion.25), channel_id=1, source_target_pairs={{0,6},{1,7},{2,0},{3,1},{4,2},{5,3},{6,4},{7,5},{8,14},{9,15},{10,... | collective-permute-start | bytes 589832 | tf_op jit(solution)/shard_map/ppermute | solution.py:13
  79.9 7.6 %collective-permute-start.21 = (bf16[128,256]{1,0:T(8,128)(2,1)S(1)}, bf16[128,256]{1,0:T(8,128)(2,1)S(1)}, u32[]{:S(2)}, u32[]{:S(2)}) collective-permute-start(bf16[128,256]{1,0:T(8,128)(2,1)S(1)} %fusion.39), channel_id=1, source_target_pairs={{0,2},{1,3},{2,4},{3,5},{4,6},{5,7},{6,0},{7,1},{8,10},{9,11},{10,... | collective-permute-start | bytes 196616 | tf_op jit(solution)/shard_map/ppermute | solution.py:13
  80.1 7.6 %collective-permute-start.20 = (bf16[128,256]{1,0:T(8,128)(2,1)S(1)}, bf16[128,256]{1,0:T(8,128)(2,1)S(1)}, u32[]{:S(2)}, u32[]{:S(2)}) collective-permute-start(bf16[128,256]{1,0:T(8,128)(2,1)S(1)} %fusion.31), channel_id=1, source_target_pairs={{0,6},{1,7},{2,0},{3,1},{4,2},{5,3},{6,4},{7,5},{8,14},{9,15},{10,... | collective-permute-start | bytes 196616 | tf_op jit(solution)/shard_map/ppermute | solution.py:13
  84.0 7.5 %collective-permute-start.13 = (bf16[128,768]{1,0:T(8,128)(2,1)S(1)}, bf16[128,768]{1,0:T(8,128)(2,1)S(1)}, u32[]{:S(2)}, u32[]{:S(2)}) collective-permute-start(bf16[128,768]{1,0:T(8,128)(2,1)S(1)} %fusion.17), channel_id=1, source_target_pairs={{0,2},{1,3},{2,4},{3,5},{4,6},{5,7},{6,0},{7,1},{8,10},{9,11},{10,... | collective-permute-start | bytes 589832 | tf_op jit(solution)/shard_map/ppermute | solution.py:13
  121.4 3.8 %copy-start.2 = (f32[8192]{0:T(1024)S(1)}, f32[8192]{0:T(1024)}, u32[]{:S(2)}) copy-start(f32[8192]{0:T(1024)} %param.7) | copy-start | bytes 98308

commit v2 on v1

--- a/solution.py
+++ b/solution.py
@@ -30,25 +30,32 @@
     return lax.optimization_barrier((value,) + earlier)[0]
 
 
-def reduce_z(part, place, sign, earlier):
+def mirror(value, step):
+    n_b, n_t = lax.axis_size("batch"), lax.axis_size("tensor")
+    pairs = [
+        (b * n_t + t, b * n_t + (t + (step if b % 2 == 0 else -step)) % n_t)
+        for b in range(n_b)
+        for t in range(n_t)
+    ]
+    return lax.ppermute(value, ("batch", "tensor"), pairs)
+
+
+def reduce_z(part, place, sign):
     def block(r):
         return lax.dynamic_index_in_dim(part, place(r), 0, keepdims=False)
 
     def pair(p, q):
         return jnp.stack([block(p).astype(BF16), block(q).astype(BF16)])
 
-    ahead, behind, last = pair(3 * sign, sign), pair(-3 * sign, -sign), block(4).astype(BF16)
-    if earlier:
-        ahead, behind, last = after(ahead, *earlier), after(behind, *earlier), after(last, *earlier)
-    near = shift(ahead, "tensor", sign).astype(F32)
-    far = shift(last, "tensor", 2 * sign).astype(F32)
-    back = shift(behind, "tensor", -sign).astype(F32)
+    near = mirror(pair(3 * sign, sign), sign).astype(F32)
+    far = mirror(block(4).astype(BF16), 2 * sign).astype(F32)
+    back = mirror(pair(-3 * sign, -sign), -sign).astype(F32)
     first = (block(2 * sign) + near[0] + far).astype(BF16)
     second = (block(-2 * sign) + back[0]).astype(BF16)
-    one = shift(first, "tensor", 2 * sign)
-    two = shift(second, "tensor", -2 * sign)
+    one = mirror(first, 2 * sign)
+    two = mirror(second, -2 * sign)
     total = block(0) + (near[1] + back[1]) + (one.astype(F32) + two.astype(F32))
-    return total.astype(BF16), (first, second)
+    return total.astype(BF16)
 
 
 def body(captured, fc_weight, owner, norm_gain):
@@ -86,7 +93,7 @@
     )
 
     def place(r):
-        target = (ti + r) % n_tensor
+        target = (ti + r * (1 - 2 * ci)) % n_tensor
         return ((target // 2 - yi) % (n_batch // 2)) * 2 + (target % 2 ^ ci)
 
     mine = lax.dynamic_index_in_dim(
@@ -94,30 +101,31 @@
     )
     table = slot_table(mine, owners, slot_cap)
 
-    def job(weights, sign, earlier):
+    def job(weights, sign):
         weight = jnp.concatenate(weights, axis=2)
         part = jnp.einsum("lnk,lkc->nc", tokens, weight, preferred_element_type=F32)
         part = part.reshape(n_batch, rows, weight.shape[2])
-        return reduce_z(part, place, sign, earlier)
+        return reduce_z(part, place, sign)
 
-    first, _ = job([fc_weight, w_up, w_dn], 1, ())
-    second, _ = job([far_a, far_b], -1, ())
+    first = job([fc_weight, w_up, w_dn], 1)
+    second = job([far_a, far_b], -1)
     done = [first, second]
-    merged = jnp.concatenate(done, axis=1)
+    here = jnp.concatenate(
+        [first[:, :col], first[:, 2 * col :], second, first[:, col : 2 * col]], axis=1
+    )
+    merged = lax.dynamic_slice_in_dim(
+        jnp.concatenate([here, here], axis=1), (n_section - si) % n_section * col, n_section * col, 1
+    )
     outgoing = jnp.einsum("rom,rc->omc", table, merged, preferred_element_type=F32).astype(BF16)
     incoming = lax.all_to_all(
         outgoing, ("section", "batch"), split_axis=0, concat_axis=0, tiled=True
     )
-    incoming = incoming.reshape(n_section, n_batch, slot_cap, n_section, col)
-    rows_of = []
-    for s in range(n_section):
-        order = {(s + d) % n_section: i for i, d in enumerate((0, -1, 1, 2))}
-        parts = [incoming[s, :, :, order[p]] for p in range(n_section)]
-        rows_of.append(jnp.stack(parts, axis=2).transpose(1, 0, 2, 3).reshape(slot_cap, width))
-    values = jnp.stack(rows_of, axis=1).astype(F32)
-    square_mean = jnp.mean(values * values, axis=-1, keepdims=True)
-    normed = (values * lax.rsqrt(square_mean + 1e-05) * norm_gain).astype(BF16)
-    return normed.transpose(1, 0, 2)[None, None]
+    values = incoming.reshape(n_section, n_batch, slot_cap, n_section * col)
+    wide = values.astype(F32)
+    square_mean = jnp.sum(wide * wide, axis=(1, 3), keepdims=True) / width
+    gain = norm_gain.reshape(1, n_batch, 1, n_section * col)
+    normed = (wide * lax.rsqrt(square_mean + 1e-05) * gain).astype(BF16)
+    return normed.transpose(0, 2, 1, 3).reshape(1, 1, n_section, slot_cap, width)
 
 
 def solution(mesh):

time: 127 us -> 119 us (0.937)
  blocking collectives: 29 us -> 0 us
  starting transfers between devices: 40.2 us -> 52.1 us
  waiting for transfers between devices: 30.5 us -> 40.7 us
  local copies, waits for them, and re-layouts: 13.2 us -> 11.5 us
    all_to_all x1 -> x0, blocking collectives: 29 us -> none  [body(): lax.all_to_all(outgoing, ('section', 'batch'), split_axis=0, concat_axis=...]
    ppermute x0 -> x10, starting transfers between devices: none -> 23.5 us  [mirror(): return lax.ppermute(value, ('batch', 'tensor'), pairs)]
    ppermute x14 -> x4, starting transfers between devices: 26.2 us -> 6.14 us  [shift(): return lax.ppermute(value, axis, [(i, (i + step) % n) for i in range(n)])]
    all_to_all x0 -> x1, waiting for transfers between devices: none -> 16.9 us  [body(): lax.all_to_all(outgoing, ('section', 'batch'), split_axis=0, concat_axis=...]
    ppermute x14 -> x4, waiting for transfers between devices: 17 us -> 0.79 us  [shift(): return lax.ppermute(value, axis, [(i, (i + step) % n) for i in range(n)])]
    ppermute x0 -> x10, waiting for transfers between devices: none -> 9.68 us  [mirror(): return lax.ppermute(value, ('batch', 'tensor'), pairs)]
    all_to_all x0 -> x1, starting transfers between devices: none -> 8.47 us  [body(): lax.all_to_all(outgoing, ('section', 'batch'), split_axis=0, concat_axis=...]
    slice x1 -> x0, local copies, waits for them, and re-layouts: 1.58 us -> none  [body(): parts = [incoming[s, :, :, order[p]] for p in range(n_section)]]
  transfers between devices with their start and end apart: 22 -> 23, of which waited for: 8 -> 10; matrix products, arithmetic and copies ran while one was open for 16% -> 17% of each run, Pallas kernels for 0% -> 0%
where the time goes in v2:
time: 119 us; the launch traced here: 118 us
  starting transfers between devices  52.1 us (44%)
  waiting for transfers between devices  40.7 us (34%)
  local copies, waits for them, and re-layouts  11.5 us (10%)
  matrix products  9.06 us (8%)
  other arithmetic  4.5 us (4%)
    ppermute x10, starting transfers between devices, mirror(): return lax.ppermute(value, ('batch', 'tensor'), pairs)  23.5 us
    all_to_all x1, waiting for transfers between devices, body(): lax.all_to_all(outgoing, ('section', 'batch'), split_axis=0, concat_axis=...  16.9 us
    ppermute x8, starting transfers between devices, hop(): return lax.ppermute(value, 'batch', pairs)  14 us
    ppermute x8, waiting for transfers between devices, hop(): return lax.ppermute(value, 'batch', pairs)  13.3 us
    ppermute x10, waiting for transfers between devices, mirror(): return lax.ppermute(value, ('batch', 'tensor'), pairs)  9.68 us
    dot_general x2, matrix products, job(): part = jnp.einsum('lnk,lkc->nc', tokens, weight, preferred_element_type=F32)  8.7 us
    all_to_all x1, starting transfers between devices, body(): lax.all_to_all(outgoing, ('section', 'batch'), split_axis=0, concat_axis=...  8.47 us
    ppermute x4, starting transfers between devices, shift(): return lax.ppermute(value, axis, [(i, (i + step) % n) for i in range(n)])  6.14 us
  transfers between devices with their start and end apart: 23, of which 10 were waited for; matrix products, arithmetic and copies ran while one was open for 17% of the time, Pallas kernels for 0%

profile of v2, /device:TPU:1, one launch (start us, length us, event | category | flops | bytes accessed | tf_op | source)
XLA Modules:
  0.0 118.2 jit_solution(14402798263278162910)
XLA Ops:
  0.0 2.1 %collective-permute-start.3 = (bf16[3,128,1024]{2,1,0:T(8,128)(2,1)}, bf16[3,128,1024]{2,1,0:T(8,128)(2,1)S(1)}, u32[]{:S(2)}, u32[]{:S(2)}) collective-permute-start(bf16[3,128,1024]{2,1,0:T(8,128)(2,1)} %bitcast.65), channel_id=1, source_target_pairs={{0,16},{8,24},{16,32},{24,40},{32,48},{40,56},{48,0},{56,8},{1,17}... | collective-permute-start | bytes 2359304 | tf_op jit(solution)/shard_map/ppermute | solution.py:19
  2.1 1.5 %collective-permute-start.1 = (bf16[3,128,1024]{2,1,0:T(8,128)(2,1)}, bf16[3,128,1024]{2,1,0:T(8,128)(2,1)S(1)}, u32[]{:S(2)}, u32[]{:S(2)}) collective-permute-start(bf16[3,128,1024]{2,1,0:T(8,128)(2,1)} %bitcast.66), channel_id=1, source_target_pairs={{0,48},{8,56},{16,0},{24,8},{32,16},{40,24},{48,32},{56,40},{1,49}... | collective-permute-start | bytes 2359304 | tf_op jit(solution)/shard_map/ppermute | solution.py:19
  3.7 1.2 %collective-permute-start.8 = (bf16[3,1024,256]{2,1,0:T(8,128)(2,1)}, bf16[3,1024,256]{2,1,0:T(8,128)(2,1)}, u32[]{:S(2)}, u32[]{:S(2)}) collective-permute-start(bf16[3,1024,256]{2,1,0:T(8,128)(2,1)} %param.5), channel_id=1, source_target_pairs={{0,64},{64,128},{128,192},{192,0},{1,65},{65,129},{129,193},{193,1... | collective-permute-start | bytes 4718600 | tf_op jit(solution)/shard_map/ppermute | solution.py:13
  4.9 1.5 %collective-permute-start.9 = (bf16[3,1024,256]{2,1,0:T(8,128)(2,1)}, bf16[3,1024,256]{2,1,0:T(8,128)(2,1)}, u32[]{:S(2)}, u32[]{:S(2)}) collective-permute-start(bf16[3,1024,256]{2,1,0:T(8,128)(2,1)} %param.5), channel_id=1, source_target_pairs={{0,192},{64,0},{128,64},{192,128},{1,193},{65,1},{129,65},{193,129... | collective-permute-start | bytes 4718600 | tf_op jit(solution)/shard_map/ppermute | solution.py:13
  6.3 12.8 %collective-permute-done.3 = bf16[3,128,1024]{2,1,0:T(8,128)(2,1)S(1)} collective-permute-done((bf16[3,128,1024]{2,1,0:T(8,128)(2,1)}, bf16[3,128,1024]{2,1,0:T(8,128)(2,1)S(1)}, u32[]{:S(2)}, u32[]{:S(2)}) %collective-permute-start.3) | collective-permute-done | bytes 786464 | tf_op jit(solution)/shard_map/ppermute | solution.py:19
  19.1 1.6 %collective-permute-start.4 = (bf16[3,64,1024]{2,1,0:T(8,128)(2,1)S(1)}, bf16[3,64,1024]{2,1,0:T(8,128)(2,1)S(1)}, u32[]{:S(2)}, u32[]{:S(2)}) collective-permute-start(bf16[3,64,1024]{2,1,0:T(8,128)(2,1)S(1)} %slice.60), channel_id=1, source_target_pairs={{0,16},{8,24},{16,32},{24,40},{32,48},{40,56},{48,0},{56,8},{1,17}... | collective-permute-start | bytes 1179656 | tf_op jit(solution)/shard_map/ppermute | solution.py:19
  20.8 1.9 %collective-permute-start = (bf16[3,128,1024]{2,1,0:T(8,128)(2,1)}, bf16[3,128,1024]{2,1,0:T(8,128)(2,1)S(1)}, u32[]{:S(2)}, u32[]{:S(2)}) collective-permute-start(bf16[3,128,1024]{2,1,0:T(8,128)(2,1)} %bitcast.67), channel_id=1, source_target_pairs={{0,8},{8,0},{16,24},{24,16},{32,40},{40,32},{48,56},{56,48},{1,9},... | collective-permute-start | bytes 2359304 | tf_op jit(solution)/shard_map/ppermute | solution.py:19
  22.7 0.8 slice.61
  23.5 2.7 %collective-permute-start.5 = (bf16[3,64,1024]{2,1,0:T(8,128)(2,1)}, bf16[3,64,1024]{2,1,0:T(8,128)(2,1)S(1)}, u32[]{:S(2)}, u32[]{:S(2)}) collective-permute-start(bf16[3,64,1024]{2,1,0:T(8,128)(2,1)} %slice.61), channel_id=1, source_target_pairs={{0,48},{8,56},{16,0},{24,8},{32,16},{40,24},{48,32},{56,40},{1,49}... | collective-permute-start | bytes 1179656 | tf_op jit(solution)/shard_map/ppermute | solution.py:19
  26.1 0.7 broadcast_compare_fusion
  26.8 1.6 %reduce_window_sum.11 = s32[128,32]{1,0:T(8,128)} reduce-window(s32[128,32]{1,0:T(8,128)} %get-tuple-element.18, s32[]{:T(128)} %constant.319.clone.1), window={size=128x1 pad=127_0x0_0}, to_apply=%region_0.1 | reduce-window | flops 520192 | bytes 32772 | tf_op jit(solution)/shard_map/jit(cumsum)/reduce_window_sum | solution.py:24
  28.4 0.6 collective-permute-done.4
  29.0 3.5 %collective-permute-start.2 = (bf16[3,128,1024]{2,1,0:T(8,128)(2,1)S(1)}, bf16[3,128,1024]{2,1,0:T(8,128)(2,1)}, u32[]{:S(2)}, u32[]{:S(2)}) collective-permute-start(bf16[3,128,1024]{2,1,0:T(8,128)(2,1)S(1)} %collective-permute-done.1), channel_id=1, source_target_pairs={{0,8},{8,0},{16,24},{24,16},{32,40},{40,32},{48,56},{56,48},{1,9},... | collective-permute-start | bytes 2359304 | tf_op jit(solution)/shard_map/ppermute | solution.py:19
  32.5 0.8 broadcast_add_fusion
  33.3 0.7 copy.12
  34.0 1.4 %copy.13 = pred[128,32]{0,1:T(8,128)(4,1)} copy(pred[128,32]{1,0:T(8,128)(4,1)} %get-tuple-element.17) | data formatting | bytes 8192 | tf_op jit(solution)/shard_map/eq | solution.py:25
  35.4 0.5 collective-permute-start.6
  35.9 1.2 %constant_dynamic-update-slice_fusion.8 = bf16[3,1024,1024]{2,1,0:T(8,128)(2,1)S(1)} fusion(bf16[128,3,1024]{2,0,1:T(8,128)(2,1)} %param.4), kind=kLoop, calls=%fused_computation.77 | loop fusion | bytes 1572864
  37.5 0.8 collective-permute-done.8
  38.2 1.2 %slice.68 = bf16[3,1024,128]{2,1,0:T(8,128)(2,1)S(1)} slice(bf16[3,1024,256]{2,1,0:T(8,128)(2,1)} %collective-permute-done.8), slice={[0:3], [0:1024], [0:128]} | slice | bytes 1572864 | tf_op jit(solution)/shard_map/slice | solution.py:87
  39.4 1.8 %collective-permute-start.15 = (bf16[3,1024,128]{2,1,0:T(8,128)(2,1)S(1)}, bf16[3,1024,128]{2,1,0:T(8,128)(2,1)S(1)}, u32[]{:S(2)}, u32[]{:S(2)}) collective-permute-start(bf16[3,1024,128]{2,1,0:T(8,128)(2,1)S(1)} %slice.68), channel_id=1, source_target_pairs={{0,64},{64,128},{128,192},{192,0},{1,65},{65,129},{129,193},{193,1... | collective-permute-start | bytes 2359304 | tf_op jit(solution)/shard_map/ppermute | solution.py:13
  41.2 1.2 %slice.69 = bf16[3,1024,128]{2,1,0:T(8,128)(2,1)S(1)} slice(bf16[3,1024,256]{2,1,0:T(8,128)(2,1)} %collective-permute-done.9), slice={[0:3], [0:1024], [128:256]} | slice | bytes 1572864 | tf_op jit(solution)/shard_map/slice | solution.py:88
  42.4 1.7 %collective-permute-start.16 = (bf16[3,1024,128]{2,1,0:T(8,128)(2,1)S(1)}, bf16[3,1024,128]{2,1,0:T(8,128)(2,1)S(1)}, u32[]{:S(2)}, u32[]{:S(2)}) collective-permute-start(bf16[3,1024,128]{2,1,0:T(8,128)(2,1)S(1)} %slice.69), channel_id=1, source_target_pairs={{0,192},{64,0},{128,64},{192,128},{1,193},{65,1},{129,65},{193,129... | collective-permute-start | bytes 2359304 | tf_op jit(solution)/shard_map/ppermute | solution.py:13
  44.1 1.2 %constant_dynamic-update-slice_fusion.5 = bf16[3,1024,1024]{2,1,0:T(8,128)(2,1)S(1)} fusion(bf16[3,1024,1024]{2,1,0:T(8,128)(2,1)S(1)} %constant_dynamic-update-slice_fusion.6, bf16[3,128,1024]{2,1,0:T(8,128)(2,1)} %collective-permute-done.2), kind=kLoop, calls=%fused_computation.74 | loop fusion | bytes 1572864
  45.5 6.9 %fusion = f32[1024,768,1]{1,0,2:T(8,128)S(1)} fusion(bf16[3,1024,1024]{2,1,0:T(8,128)(2,1)S(1)} %constant_dynamic-update-slice_fusion, bf16[3,1024,256]{2,1,0:T(8,128)(2,1)} %collective-permute-done.9, bf16[3,1024,256]{2,1,0:T(8,128)(2,1)} %collective-permute-done.8, bf16[3,1024,256]{2,1,0:T(8,128)(2,1)S(1)} %copy-done.4), kind=kOutput, calls=%fused_computation | convolution fusion | flops 4845993984 | bytes 14155776 | tf_op jit(solution)/shard_map/lnk,lkc->nc/dot_general | solution.py:106
  52.6 6.9 %collective-permute-start.10 = (bf16[2,128,768]{2,1,0:T(8,128)(2,1)S(1)}, bf16[2,128,768]{2,1,0:T(8,128)(2,1)S(1)}, u32[]{:S(2)}, u32[]{:S(2)}) collective-permute-start(bf16[2,128,768]{2,1,0:T(8,128)(2,1)S(1)} %pad_maximum_fusion.1), channel_id=1, source_target_pairs={{0,1},{1,2},{2,3},{3,4},{4,5},{5,6},{6,7},{7,0},{8,15},{9,8},{10,9... | collective-permute-start | bytes 1179656 | tf_op jit(solution)/shard_map/ppermute | solution.py:40
  59.6 1.2 collective-permute-start.12
  60.8 0.8 collective-permute-start.11
  61.6 1.8 %fusion.6 = f32[1024,256,1]{1,0,2:T(8,128)S(1)} fusion(bf16[3,1024,1024]{2,1,0:T(8,128)(2,1)S(1)} %constant_dynamic-update-slice_fusion, bf16[3,1024,128]{2,1,0:T(8,128)(2,1)S(1)} %collective-permute-done.16, bf16[3,1024,128]{2,1,0:T(8,128)(2,1)S(1)} %collective-permute-done.15), kind=kOutput, calls=%fused_computation.8 | convolution fusion | flops 1613758464 | bytes 8912896 | tf_op jit(solution)/shard_map/lnk,lkc->nc/dot_general | solution.py:106
  63.5 0.8 collective-permute-start.17
  64.3 2.2 %collective-permute-start.19 = (bf16[128,256]{1,0:T(8,128)(2,1)S(1)}, bf16[128,256]{1,0:T(8,128)(2,1)S(1)}, u32[]{:S(2)}, u32[]{:S(2)}) collective-permute-start(bf16[128,256]{1,0:T(8,128)(2,1)S(1)} %get-tuple-element.12), channel_id=1, source_target_pairs={{0,6},{1,7},{2,0},{3,1},{4,2},{5,3},{6,4},{7,5},{8,10},{9,11},{10,... | collective-permute-start | bytes 196616 | tf_op jit(solution)/shard_map/ppermute | solution.py:40
  66.5 1.6 %collective-permute-done.10 = bf16[2,128,768]{2,1,0:T(8,128)(2,1)S(1)} collective-permute-done((bf16[2,128,768]{2,1,0:T(8,128)(2,1)S(1)}, bf16[2,128,768]{2,1,0:T(8,128)(2,1)S(1)}, u32[]{:S(2)}, u32[]{:S(2)}) %collective-permute-start.10) | collective-permute-done | bytes 393248 | tf_op jit(solution)/shard_map/ppermute | solution.py:40
  68.1 3.4 %collective-permute-start.18 = (bf16[2,128,256]{2,1,0:T(8,128)(2,1)S(1)}, bf16[2,128,256]{2,1,0:T(8,128)(2,1)S(1)}, u32[]{:S(2)}, u32[]{:S(2)}) collective-permute-start(bf16[2,128,256]{2,1,0:T(8,128)(2,1)S(1)} %pad_maximum_fusion.4), channel_id=1, source_target_pairs={{0,1},{1,2},{2,3},{3,4},{4,5},{5,6},{6,7},{7,0},{8,15},{9,8},{10,9... | collective-permute-start | bytes 393224 | tf_op jit(solution)/shard_map/ppermute | solution.py:40
  71.6 0.7 collective-permute-done.12
  72.4 4.1 %collective-permute-start.13 = (bf16[128,768]{1,0:T(8,128)(2,1)S(1)}, bf16[128,768]{1,0:T(8,128)(2,1)S(1)}, u32[]{:S(2)}, u32[]{:S(2)}) collective-permute-start(bf16[128,768]{1,0:T(8,128)(2,1)S(1)} %fusion.14), channel_id=1, source_target_pairs={{0,2},{1,3},{2,4},{3,5},{4,6},{5,7},{6,0},{7,1},{8,14},{9,15},{10,... | collective-permute-start | bytes 589832 | tf_op jit(solution)/shard_map/ppermute | solution.py:40
  76.7 0.5 collective-permute-done.17
  77.2 0.7 collective-permute-done.19
  77.9 0.5 collective-permute-start.20
  78.4 3.5 %collective-permute-start.21 = (bf16[128,256]{1,0:T(8,128)(2,1)S(1)}, bf16[128,256]{1,0:T(8,128)(2,1)S(1)}, u32[]{:S(2)}, u32[]{:S(2)}) collective-permute-start(bf16[128,256]{1,0:T(8,128)(2,1)S(1)} %fusion.36), channel_id=1, source_target_pairs={{0,2},{1,3},{2,4},{3,5},{4,6},{5,7},{6,0},{7,1},{8,14},{9,15},{10,... | collective-permute-start | bytes 196616 | tf_op jit(solution)/shard_map/ppermute | solution.py:40
  81.9 3.6 %collective-permute-done.14 = bf16[128,768]{1,0:T(8,128)(2,1)S(1)} collective-permute-done((bf16[128,768]{1,0:T(8,128)(2,1)S(1)}, bf16[128,768]{1,0:T(8,128)(2,1)S(1)}, u32[]{:S(2)}, u32[]{:S(2)}) %collective-permute-start.14) | collective-permute-done | bytes 196640 | tf_op jit(solution)/shard_map/ppermute | solution.py:40
  85.6 2.6 %collective-permute-done.20 = bf16[128,256]{1,0:T(8,128)(2,1)S(1)} collective-permute-done((bf16[128,256]{1,0:T(8,128)(2,1)S(1)}, bf16[128,256]{1,0:T(8,128)(2,1)S(1)}, u32[]{:S(2)}, u32[]{:S(2)}) %collective-permute-start.20) | collective-permute-done | bytes 65568 | tf_op jit(solution)/shard_map/ppermute | solution.py:40
  88.4 0.4 convolution_convert_fusion
  88.7 1.4 %copy.14 = bf16[32,12,1024]{2,1,0:T(8,128)(2,1)} copy(bf16[32,12,1024]{2,0,1:T(8,128)(2,1)S(1)} %convolution_convert_fusion) | data formatting | bytes 1572864 | tf_op jit(solution)/shard_map/convert_element_type | solution.py:119
  90.2 8.5 %all-to-all-start = ((bf16[32,12,1024]{2,1,0:T(8,128)(2,1)}), bf16[32,12,1024]{2,1,0:T(8,128)(2,1)S(1)}, u32[]{:S(2)}, u32[]{:S(2)}) async-start(bf16[32,12,1024]{2,1,0:T(8,128)(2,1)} %copy.14), calls=%async_computation | async-start | bytes 2097152 | tf_op jit(solution)/shard_map/all_to_all | solution.py:120
  98.7 16.9 %all-to-all-done = bf16[32,12,1024]{2,1,0:T(8,128)(2,1)S(1)} async-done(((bf16[32,12,1024]{2,1,0:T(8,128)(2,1)}), bf16[32,12,1024]{2,1,0:T(8,128)(2,1)S(1)}, u32[]{:S(2)}, u32[]{:S(2)}) %all-to-all-start) | async-done | bytes 786464 | tf_op jit(solution)/shard_map/all_to_all | solution.py:120
  115.9 0.4 fusion.10
  116.3 0.4 copy.17
  116.7 1.5 %reshape.93 = bf16[1,1,4,12,8192]{4,2,3,1,0:T(4,128)(2,1)} reshape(bf16[4,12,8,1024]{3,2,0,1:T(8,128)(2,1)S(1)} %copy.17) | data formatting | bytes 1572864 | tf_op jit(solution)/shard_map/reshape | solution.py:128
  (62 shorter events, 1.9 us)
Async XLA Ops:
  0.0 22.7 %copy-start = (s32[4096,1]{0,1:T(1,128)S(1)}, s32[4096,1]{0,1:T(1,128)}, u32[]{:S(2)}) copy-start(s32[4096,1]{0,1:T(1,128)} %param.6) | copy-start | bytes 49156
  0.0 19.1 %collective-permute-start.3 = (bf16[3,128,1024]{2,1,0:T(8,128)(2,1)}, bf16[3,128,1024]{2,1,0:T(8,128)(2,1)S(1)}, u32[]{:S(2)}, u32[]{:S(2)}) collective-permute-start(bf16[3,128,1024]{2,1,0:T(8,128)(2,1)} %bitcast.65), channel_id=1, source_target_pairs={{0,16},{8,24},{16,32},{24,40},{32,48},{40,56},{48,0},{56,8},{1,17}... | collective-permute-start | bytes 2359304 | tf_op jit(solution)/shard_map/ppermute | solution.py:19
  2.1 20.6 %collective-permute-start.1 = (bf16[3,128,1024]{2,1,0:T(8,128)(2,1)}, bf16[3,128,1024]{2,1,0:T(8,128)(2,1)S(1)}, u32[]{:S(2)}, u32[]{:S(2)}) collective-permute-start(bf16[3,128,1024]{2,1,0:T(8,128)(2,1)} %bitcast.66), channel_id=1, source_target_pairs={{0,48},{8,56},{16,0},{24,8},{32,16},{40,24},{48,32},{56,40},{1,49}... | collective-permute-start | bytes 2359304 | tf_op jit(solution)/shard_map/ppermute | solution.py:19
  3.7 34.6 %collective-permute-start.8 = (bf16[3,1024,256]{2,1,0:T(8,128)(2,1)}, bf16[3,1024,256]{2,1,0:T(8,128)(2,1)}, u32[]{:S(2)}, u32[]{:S(2)}) collective-permute-start(bf16[3,1024,256]{2,1,0:T(8,128)(2,1)} %param.5), channel_id=1, source_target_pairs={{0,64},{64,128},{128,192},{192,0},{1,65},{65,129},{129,193},{193,1... | collective-permute-start | bytes 4718600 | tf_op jit(solution)/shard_map/ppermute | solution.py:13
  4.9 36.4 %collective-permute-start.9 = (bf16[3,1024,256]{2,1,0:T(8,128)(2,1)}, bf16[3,1024,256]{2,1,0:T(8,128)(2,1)}, u32[]{:S(2)}, u32[]{:S(2)}) collective-permute-start(bf16[3,1024,256]{2,1,0:T(8,128)(2,1)} %param.5), channel_id=1, source_target_pairs={{0,192},{64,0},{128,64},{192,128},{1,193},{65,1},{129,65},{193,129... | collective-permute-start | bytes 4718600 | tf_op jit(solution)/shard_map/ppermute | solution.py:13
  19.1 9.9 %collective-permute-start.4 = (bf16[3,64,1024]{2,1,0:T(8,128)(2,1)S(1)}, bf16[3,64,1024]{2,1,0:T(8,128)(2,1)S(1)}, u32[]{:S(2)}, u32[]{:S(2)}) collective-permute-start(bf16[3,64,1024]{2,1,0:T(8,128)(2,1)S(1)} %slice.60), channel_id=1, source_target_pairs={{0,16},{8,24},{16,32},{24,40},{32,48},{40,56},{48,0},{56,8},{1,17}... | collective-permute-start | bytes 1179656 | tf_op jit(solution)/shard_map/ppermute | solution.py:19
  20.8 16.3 %collective-permute-start = (bf16[3,128,1024]{2,1,0:T(8,128)(2,1)}, bf16[3,128,1024]{2,1,0:T(8,128)(2,1)S(1)}, u32[]{:S(2)}, u32[]{:S(2)}) collective-permute-start(bf16[3,128,1024]{2,1,0:T(8,128)(2,1)} %bitcast.67), channel_id=1, source_target_pairs={{0,8},{8,0},{16,24},{24,16},{32,40},{40,32},{48,56},{56,48},{1,9},... | collective-permute-start | bytes 2359304 | tf_op jit(solution)/shard_map/ppermute | solution.py:19
  23.5 11.9 %collective-permute-start.5 = (bf16[3,64,1024]{2,1,0:T(8,128)(2,1)}, bf16[3,64,1024]{2,1,0:T(8,128)(2,1)S(1)}, u32[]{:S(2)}, u32[]{:S(2)}) collective-permute-start(bf16[3,64,1024]{2,1,0:T(8,128)(2,1)} %slice.61), channel_id=1, source_target_pairs={{0,48},{8,56},{16,0},{24,8},{32,16},{40,24},{48,32},{56,40},{1,49}... | collective-permute-start | bytes 1179656 | tf_op jit(solution)/shard_map/ppermute | solution.py:19
  29.0 15.1 %collective-permute-start.2 = (bf16[3,128,1024]{2,1,0:T(8,128)(2,1)S(1)}, bf16[3,128,1024]{2,1,0:T(8,128)(2,1)}, u32[]{:S(2)}, u32[]{:S(2)}) collective-permute-start(bf16[3,128,1024]{2,1,0:T(8,128)(2,1)S(1)} %collective-permute-done.1), channel_id=1, source_target_pairs={{0,8},{8,0},{16,24},{24,16},{32,40},{40,32},{48,56},{56,48},{1,9},... | collective-permute-start | bytes 2359304 | tf_op jit(solution)/shard_map/ppermute | solution.py:19
  35.4 9.9 %collective-permute-start.6 = (bf16[3,128,1024]{2,1,0:T(8,128)(2,1)S(1)}, bf16[3,128,1024]{2,1,0:T(8,128)(2,1)S(1)}, u32[]{:S(2)}, u32[]{:S(2)}) collective-permute-start(bf16[3,128,1024]{2,1,0:T(8,128)(2,1)S(1)} %pad_maximum_fusion), channel_id=1, source_target_pairs={{0,8},{8,0},{16,24},{24,16},{32,40},{40,32},{48,56},{56,48},{1,9},... | collective-permute-start | bytes 2359304 | tf_op jit(solution)/shard_map/ppermute | solution.py:19
  37.1 8.4 %collective-permute-start.7 = (bf16[3,128,1024]{2,1,0:T(8,128)(2,1)S(1)}, bf16[3,128,1024]{2,1,0:T(8,128)(2,1)S(1)}, u32[]{:S(2)}, u32[]{:S(2)}) collective-permute-start(bf16[3,128,1024]{2,1,0:T(8,128)(2,1)S(1)} %collective-permute-done.3), channel_id=1, source_target_pairs={{0,8},{8,0},{16,24},{24,16},{32,40},{40,32},{48,56},{56,48},{1,9},... | collective-permute-start | bytes 2359304 | tf_op jit(solution)/shard_map/ppermute | solution.py:19
  37.4 8.2 %copy-start.4 = (bf16[3,1024,256]{2,1,0:T(8,128)(2,1)S(1)}, bf16[3,1024,256]{2,1,0:T(8,128)(2,1)}, u32[]{:S(2)}) copy-start(bf16[3,1024,256]{2,1,0:T(8,128)(2,1)} %param.5) | copy-start | bytes 4718596
  39.4 22.2 %collective-permute-start.15 = (bf16[3,1024,128]{2,1,0:T(8,128)(2,1)S(1)}, bf16[3,1024,128]{2,1,0:T(8,128)(2,1)S(1)}, u32[]{:S(2)}, u32[]{:S(2)}) collective-permute-start(bf16[3,1024,128]{2,1,0:T(8,128)(2,1)S(1)} %slice.68), channel_id=1, source_target_pairs={{0,64},{64,128},{128,192},{192,0},{1,65},{65,129},{129,193},{193,1... | collective-permute-start | bytes 2359304 | tf_op jit(solution)/shard_map/ppermute | solution.py:13
  42.4 19.2 %collective-permute-start.16 = (bf16[3,1024,128]{2,1,0:T(8,128)(2,1)S(1)}, bf16[3,1024,128]{2,1,0:T(8,128)(2,1)S(1)}, u32[]{:S(2)}, u32[]{:S(2)}) collective-permute-start(bf16[3,1024,128]{2,1,0:T(8,128)(2,1)S(1)} %slice.69), channel_id=1, source_target_pairs={{0,192},{64,0},{128,64},{192,128},{1,193},{65,1},{129,65},{193,129... | collective-permute-start | bytes 2359304 | tf_op jit(solution)/shard_map/ppermute | solution.py:13
  52.6 15.5 %collective-permute-start.10 = (bf16[2,128,768]{2,1,0:T(8,128)(2,1)S(1)}, bf16[2,128,768]{2,1,0:T(8,128)(2,1)S(1)}, u32[]{:S(2)}, u32[]{:S(2)}) collective-permute-start(bf16[2,128,768]{2,1,0:T(8,128)(2,1)S(1)} %pad_maximum_fusion.1), channel_id=1, source_target_pairs={{0,1},{1,2},{2,3},{3,4},{4,5},{5,6},{6,7},{7,0},{8,15},{9,8},{10,9... | collective-permute-start | bytes 1179656 | tf_op jit(solution)/shard_map/ppermute | solution.py:40
  59.6 12.8 %collective-permute-start.12 = (bf16[128,768]{1,0:T(8,128)(2,1)S(1)}, bf16[128,768]{1,0:T(8,128)(2,1)S(1)}, u32[]{:S(2)}, u32[]{:S(2)}) collective-permute-start(bf16[128,768]{1,0:T(8,128)(2,1)S(1)} %get-tuple-element.7), channel_id=1, source_target_pairs={{0,2},{1,3},{2,4},{3,5},{4,6},{5,7},{6,0},{7,1},{8,14},{9,15},{10,... | collective-permute-start | bytes 589832 | tf_op jit(solution)/shard_map/ppermute | solution.py:40
  60.8 15.7 %collective-permute-start.11 = (bf16[2,128,768]{2,1,0:T(8,128)(2,1)S(1)}, bf16[2,128,768]{2,1,0:T(8,128)(2,1)S(1)}, u32[]{:S(2)}, u32[]{:S(2)}) collective-permute-start(bf16[2,128,768]{2,1,0:T(8,128)(2,1)S(1)} %pad_maximum_fusion.2), channel_id=1, source_target_pairs={{0,7},{1,0},{2,1},{3,2},{4,3},{5,4},{6,5},{7,6},{8,9},{9,10},{10,1... | collective-permute-start | bytes 1179656 | tf_op jit(solution)/shard_map/ppermute | solution.py:40
  63.4 24.9 %copy-start.1 = (s32[128,32]{0,1:T(8,128)S(1)}, s32[128,32]{0,1:T(8,128)}, u32[]{:S(2)}) copy-start(s32[128,32]{0,1:T(8,128)} %copy.12) | copy-start | bytes 49156
  63.4 24.9 %copy-start.3 = (pred[128,32]{0,1:T(8,128)(4,1)S(1)}, pred[128,32]{0,1:T(8,128)(4,1)}, u32[]{:S(2)}) copy-start(pred[128,32]{0,1:T(8,128)(4,1)} %copy.13) | copy-start | bytes 12292
  63.5 13.7 %collective-permute-start.17 = (bf16[2,128,256]{2,1,0:T(8,128)(2,1)S(1)}, bf16[2,128,256]{2,1,0:T(8,128)(2,1)S(1)}, u32[]{:S(2)}, u32[]{:S(2)}) collective-permute-start(bf16[2,128,256]{2,1,0:T(8,128)(2,1)S(1)} %pad_maximum_fusion.3), channel_id=1, source_target_pairs={{0,7},{1,0},{2,1},{3,2},{4,3},{5,4},{6,5},{7,6},{8,9},{9,10},{10,1... | collective-permute-start | bytes 393224 | tf_op jit(solution)/shard_map/ppermute | solution.py:40
  64.3 13.6 %collective-permute-start.19 = (bf16[128,256]{1,0:T(8,128)(2,1)S(1)}, bf16[128,256]{1,0:T(8,128)(2,1)S(1)}, u32[]{:S(2)}, u32[]{:S(2)}) collective-permute-start(bf16[128,256]{1,0:T(8,128)(2,1)S(1)} %get-tuple-element.12), channel_id=1, source_target_pairs={{0,6},{1,7},{2,0},{3,1},{4,2},{5,3},{6,4},{7,5},{8,10},{9,11},{10,... | collective-permute-start | bytes 196616 | tf_op jit(solution)/shard_map/ppermute | solution.py:40
  68.1 10.3 %collective-permute-start.18 = (bf16[2,128,256]{2,1,0:T(8,128)(2,1)S(1)}, bf16[2,128,256]{2,1,0:T(8,128)(2,1)S(1)}, u32[]{:S(2)}, u32[]{:S(2)}) collective-permute-start(bf16[2,128,256]{2,1,0:T(8,128)(2,1)S(1)} %pad_maximum_fusion.4), channel_id=1, source_target_pairs={{0,1},{1,2},{2,3},{3,4},{4,5},{5,6},{6,7},{7,0},{8,15},{9,8},{10,9... | collective-permute-start | bytes 393224 | tf_op jit(solution)/shard_map/ppermute | solution.py:40
  72.4 26.3 %copy-start.2 = (f32[8192]{0:T(1024)S(1)}, f32[8192]{0:T(1024)}, u32[]{:S(2)}) copy-start(f32[8192]{0:T(1024)} %param.7) | copy-start | bytes 98308
  72.4 9.5 %collective-permute-start.13 = (bf16[128,768]{1,0:T(8,128)(2,1)S(1)}, bf16[128,768]{1,0:T(8,128)(2,1)S(1)}, u32[]{:S(2)}, u32[]{:S(2)}) collective-permute-start(bf16[128,768]{1,0:T(8,128)(2,1)S(1)} %fusion.14), channel_id=1, source_target_pairs={{0,2},{1,3},{2,4},{3,5},{4,6},{5,7},{6,0},{7,1},{8,14},{9,15},{10,... | collective-permute-start | bytes 589832 | tf_op jit(solution)/shard_map/ppermute | solution.py:40
  76.6 8.8 %collective-permute-start.14 = (bf16[128,768]{1,0:T(8,128)(2,1)S(1)}, bf16[128,768]{1,0:T(8,128)(2,1)S(1)}, u32[]{:S(2)}, u32[]{:S(2)}) collective-permute-start(bf16[128,768]{1,0:T(8,128)(2,1)S(1)} %fusion.22), channel_id=1, source_target_pairs={{0,6},{1,7},{2,0},{3,1},{4,2},{5,3},{6,4},{7,5},{8,10},{9,11},{10,... | collective-permute-start | bytes 589832 | tf_op jit(solution)/shard_map/ppermute | solution.py:40
  77.9 10.3 %collective-permute-start.20 = (bf16[128,256]{1,0:T(8,128)(2,1)S(1)}, bf16[128,256]{1,0:T(8,128)(2,1)S(1)}, u32[]{:S(2)}, u32[]{:S(2)}) collective-permute-start(bf16[128,256]{1,0:T(8,128)(2,1)S(1)} %fusion.28), channel_id=1, source_target_pairs={{0,6},{1,7},{2,0},{3,1},{4,2},{5,3},{6,4},{7,5},{8,10},{9,11},{10,... | collective-permute-start | bytes 196616 | tf_op jit(solution)/shard_map/ppermute | solution.py:40
  78.4 9.8 %collective-permute-start.21 = (bf16[128,256]{1,0:T(8,128)(2,1)S(1)}, bf16[128,256]{1,0:T(8,128)(2,1)S(1)}, u32[]{:S(2)}, u32[]{:S(2)}) collective-permute-start(bf16[128,256]{1,0:T(8,128)(2,1)S(1)} %fusion.36), channel_id=1, source_target_pairs={{0,2},{1,3},{2,4},{3,5},{4,6},{5,7},{6,0},{7,1},{8,14},{9,15},{10,... | collective-permute-start | bytes 196616 | tf_op jit(solution)/shard_map/ppermute | solution.py:40
  90.2 25.4 %all-to-all-start = ((bf16[32,12,1024]{2,1,0:T(8,128)(2,1)}), bf16[32,12,1024]{2,1,0:T(8,128)(2,1)S(1)}, u32[]{:S(2)}, u32[]{:S(2)}) async-start(bf16[32,12,1024]{2,1,0:T(8,128)(2,1)} %copy.14), calls=%async_computation | async-start | bytes 2097152 | tf_op jit(solution)/shard_map/all_to_all | solution.py:120

commit v3 on v2

--- a/solution.py
+++ b/solution.py
@@ -117,15 +117,16 @@
         jnp.concatenate([here, here], axis=1), (n_section - si) % n_section * col, n_section * col, 1
     )
     outgoing = jnp.einsum("rom,rc->omc", table, merged, preferred_element_type=F32).astype(BF16)
+    outgoing = outgoing.reshape(owners, slot_cap // 4, 4, n_section * col)
     incoming = lax.all_to_all(
         outgoing, ("section", "batch"), split_axis=0, concat_axis=0, tiled=True
     )
-    values = incoming.reshape(n_section, n_batch, slot_cap, n_section * col)
+    values = incoming.reshape(n_section, n_batch, slot_cap // 4, 4, n_section * col)
     wide = values.astype(F32)
-    square_mean = jnp.sum(wide * wide, axis=(1, 3), keepdims=True) / width
-    gain = norm_gain.reshape(1, n_batch, 1, n_section * col)
+    square_mean = jnp.sum(wide * wide, axis=(1, 4), keepdims=True) / width
+    gain = norm_gain.reshape(1, n_batch, 1, 1, n_section * col)
     normed = (wide * lax.rsqrt(square_mean + 1e-05) * gain).astype(BF16)
-    return normed.transpose(0, 2, 1, 3).reshape(1, 1, n_section, slot_cap, width)
+    return normed.transpose(0, 2, 3, 1, 4).reshape(1, 1, n_section, slot_cap, width)
 
 
 def solution(mesh):

time: 119 us -> 116 us (0.975)
  waiting for transfers between devices: 40.7 us -> 38 us
    all_to_all x1, waiting for transfers between devices: 16.9 us -> 14.2 us  [body(): lax.all_to_all(outgoing, ('section', 'batch'), split_axis=0, concat_axis=...]
    reshape x1 -> x2, local copies, waits for them, and re-layouts: 1.45 us -> 2.94 us  [the longest x1 1.49 us: body(): outgoing = outgoing.reshape(owners, slot_cap // 4, 4, n_section * col)]
    convert_element_type x1 -> x0, local copies, waits for them, and re-layouts: 1.44 us -> none  [body(): jnp.einsum('rom,rc->omc', table, merged, preferred_element_type=F32)]
    unnamed x24 -> x25, local copies, waits for them, and re-layouts: 2.7 us -> 2.81 us
  transfers between devices with their start and end apart: 23 -> 23, of which waited for: 10 -> 10; matrix products, arithmetic and copies ran while one was open for 17% -> 18% of each run, Pallas kernels for 0% -> 0%
where the time goes in v3:
time: 116 us
  starting transfers between devices  52.1 us (45%)
  waiting for transfers between devices  38 us (33%)
  local copies, waits for them, and re-layouts  11.6 us (10%)
  matrix products  9.06 us (8%)
  other arithmetic  4.8 us (4%)
    ppermute x10, starting transfers between devices, mirror(): return lax.ppermute(value, ('batch', 'tensor'), pairs)  23.5 us
    all_to_all x1, waiting for transfers between devices, body(): lax.all_to_all(outgoing, ('section', 'batch'), split_axis=0, concat_axis=...  14.2 us
    ppermute x8, starting transfers between devices, hop(): return lax.ppermute(value, 'batch', pairs)  14 us
    ppermute x8, waiting for transfers between devices, hop(): return lax.ppermute(value, 'batch', pairs)  13.3 us
    ppermute x10, waiting for transfers between devices, mirror(): return lax.ppermute(value, ('batch', 'tensor'), pairs)  9.69 us
    dot_general x2, matrix products, job(): part = jnp.einsum('lnk,lkc->nc', tokens, weight, preferred_element_type=F32)  8.7 us
    all_to_all x1, starting transfers between devices, body(): lax.all_to_all(outgoing, ('section', 'batch'), split_axis=0, concat_axis=...  8.47 us
    ppermute x4, starting transfers between devices, shift(): return lax.ppermute(value, axis, [(i, (i + step) % n) for i in range(n)])  6.14 us
  transfers between devices with their start and end apart: 23, of which 10 were waited for; matrix products, arithmetic and copies ran while one was open for 18% of the time, Pallas kernels for 0%

profile of v3, /device:TPU:1, one launch (start us, length us, event | category | flops | bytes accessed | tf_op | source)
XLA Modules:
  0.0 115.9 jit_solution(17943990001791498315)
XLA Ops:
  0.0 2.1 %collective-permute-start.3 = (bf16[3,128,1024]{2,1,0:T(8,128)(2,1)}, bf16[3,128,1024]{2,1,0:T(8,128)(2,1)S(1)}, u32[]{:S(2)}, u32[]{:S(2)}) collective-permute-start(bf16[3,128,1024]{2,1,0:T(8,128)(2,1)} %bitcast.67), channel_id=1, source_target_pairs={{0,16},{8,24},{16,32},{24,40},{32,48},{40,56},{48,0},{56,8},{1,17}... | collective-permute-start | bytes 2359304 | tf_op jit(solution)/shard_map/ppermute | solution.py:19
  2.1 1.5 %collective-permute-start.1 = (bf16[3,128,1024]{2,1,0:T(8,128)(2,1)}, bf16[3,128,1024]{2,1,0:T(8,128)(2,1)S(1)}, u32[]{:S(2)}, u32[]{:S(2)}) collective-permute-start(bf16[3,128,1024]{2,1,0:T(8,128)(2,1)} %bitcast.68), channel_id=1, source_target_pairs={{0,48},{8,56},{16,0},{24,8},{32,16},{40,24},{48,32},{56,40},{1,49}... | collective-permute-start | bytes 2359304 | tf_op jit(solution)/shard_map/ppermute | solution.py:19
  3.7 1.2 %collective-permute-start.8 = (bf16[3,1024,256]{2,1,0:T(8,128)(2,1)}, bf16[3,1024,256]{2,1,0:T(8,128)(2,1)}, u32[]{:S(2)}, u32[]{:S(2)}) collective-permute-start(bf16[3,1024,256]{2,1,0:T(8,128)(2,1)} %param.5), channel_id=1, source_target_pairs={{0,64},{64,128},{128,192},{192,0},{1,65},{65,129},{129,193},{193,1... | collective-permute-start | bytes 4718600 | tf_op jit(solution)/shard_map/ppermute | solution.py:13
  4.9 1.5 %collective-permute-start.9 = (bf16[3,1024,256]{2,1,0:T(8,128)(2,1)}, bf16[3,1024,256]{2,1,0:T(8,128)(2,1)}, u32[]{:S(2)}, u32[]{:S(2)}) collective-permute-start(bf16[3,1024,256]{2,1,0:T(8,128)(2,1)} %param.5), channel_id=1, source_target_pairs={{0,192},{64,0},{128,64},{192,128},{1,193},{65,1},{129,65},{193,129... | collective-permute-start | bytes 4718600 | tf_op jit(solution)/shard_map/ppermute | solution.py:13
  6.3 12.8 %collective-permute-done.3 = bf16[3,128,1024]{2,1,0:T(8,128)(2,1)S(1)} collective-permute-done((bf16[3,128,1024]{2,1,0:T(8,128)(2,1)}, bf16[3,128,1024]{2,1,0:T(8,128)(2,1)S(1)}, u32[]{:S(2)}, u32[]{:S(2)}) %collective-permute-start.3) | collective-permute-done | bytes 786464 | tf_op jit(solution)/shard_map/ppermute | solution.py:19
  19.1 1.6 %collective-permute-start.4 = (bf16[3,64,1024]{2,1,0:T(8,128)(2,1)S(1)}, bf16[3,64,1024]{2,1,0:T(8,128)(2,1)S(1)}, u32[]{:S(2)}, u32[]{:S(2)}) collective-permute-start(bf16[3,64,1024]{2,1,0:T(8,128)(2,1)S(1)} %slice.60), channel_id=1, source_target_pairs={{0,16},{8,24},{16,32},{24,40},{32,48},{40,56},{48,0},{56,8},{1,17}... | collective-permute-start | bytes 1179656 | tf_op jit(solution)/shard_map/ppermute | solution.py:19
  20.8 1.9 %collective-permute-start = (bf16[3,128,1024]{2,1,0:T(8,128)(2,1)}, bf16[3,128,1024]{2,1,0:T(8,128)(2,1)S(1)}, u32[]{:S(2)}, u32[]{:S(2)}) collective-permute-start(bf16[3,128,1024]{2,1,0:T(8,128)(2,1)} %bitcast.69), channel_id=1, source_target_pairs={{0,8},{8,0},{16,24},{24,16},{32,40},{40,32},{48,56},{56,48},{1,9},... | collective-permute-start | bytes 2359304 | tf_op jit(solution)/shard_map/ppermute | solution.py:19
  22.7 0.8 slice.61
  23.5 2.7 %collective-permute-start.5 = (bf16[3,64,1024]{2,1,0:T(8,128)(2,1)}, bf16[3,64,1024]{2,1,0:T(8,128)(2,1)S(1)}, u32[]{:S(2)}, u32[]{:S(2)}) collective-permute-start(bf16[3,64,1024]{2,1,0:T(8,128)(2,1)} %slice.61), channel_id=1, source_target_pairs={{0,48},{8,56},{16,0},{24,8},{32,16},{40,24},{48,32},{56,40},{1,49}... | collective-permute-start | bytes 1179656 | tf_op jit(solution)/shard_map/ppermute | solution.py:19
  26.1 0.7 broadcast_compare_fusion
  26.8 1.6 %reduce_window_sum.11 = s32[128,32]{1,0:T(8,128)} reduce-window(s32[128,32]{1,0:T(8,128)} %get-tuple-element.18, s32[]{:T(128)} %constant.319.clone.1), window={size=128x1 pad=127_0x0_0}, to_apply=%region_0.1 | reduce-window | flops 520192 | bytes 32772 | tf_op jit(solution)/shard_map/jit(cumsum)/reduce_window_sum | solution.py:24
  28.4 0.6 collective-permute-done.4
  29.0 3.5 %collective-permute-start.2 = (bf16[3,128,1024]{2,1,0:T(8,128)(2,1)S(1)}, bf16[3,128,1024]{2,1,0:T(8,128)(2,1)}, u32[]{:S(2)}, u32[]{:S(2)}) collective-permute-start(bf16[3,128,1024]{2,1,0:T(8,128)(2,1)S(1)} %collective-permute-done.1), channel_id=1, source_target_pairs={{0,8},{8,0},{16,24},{24,16},{32,40},{40,32},{48,56},{56,48},{1,9},... | collective-permute-start | bytes 2359304 | tf_op jit(solution)/shard_map/ppermute | solution.py:19
  32.5 0.8 broadcast_add_fusion
  33.3 0.7 copy.12
  34.0 1.4 %copy.13 = pred[128,32]{0,1:T(8,128)(4,1)} copy(pred[128,32]{1,0:T(8,128)(4,1)} %get-tuple-element.17) | data formatting | bytes 8192 | tf_op jit(solution)/shard_map/eq | solution.py:25
  35.4 0.5 collective-permute-start.6
  35.9 1.2 %constant_dynamic-update-slice_fusion.8 = bf16[3,1024,1024]{2,1,0:T(8,128)(2,1)S(1)} fusion(bf16[128,3,1024]{2,0,1:T(8,128)(2,1)} %param.4), kind=kLoop, calls=%fused_computation.78 | loop fusion | bytes 1572864
  37.5 0.8 collective-permute-done.8
  38.2 1.2 %slice.68 = bf16[3,1024,128]{2,1,0:T(8,128)(2,1)S(1)} slice(bf16[3,1024,256]{2,1,0:T(8,128)(2,1)} %collective-permute-done.8), slice={[0:3], [0:1024], [0:128]} | slice | bytes 1572864 | tf_op jit(solution)/shard_map/slice | solution.py:87
  39.4 1.8 %collective-permute-start.15 = (bf16[3,1024,128]{2,1,0:T(8,128)(2,1)S(1)}, bf16[3,1024,128]{2,1,0:T(8,128)(2,1)S(1)}, u32[]{:S(2)}, u32[]{:S(2)}) collective-permute-start(bf16[3,1024,128]{2,1,0:T(8,128)(2,1)S(1)} %slice.68), channel_id=1, source_target_pairs={{0,64},{64,128},{128,192},{192,0},{1,65},{65,129},{129,193},{193,1... | collective-permute-start | bytes 2359304 | tf_op jit(solution)/shard_map/ppermute | solution.py:13
  41.2 1.2 %slice.69 = bf16[3,1024,128]{2,1,0:T(8,128)(2,1)S(1)} slice(bf16[3,1024,256]{2,1,0:T(8,128)(2,1)} %collective-permute-done.9), slice={[0:3], [0:1024], [128:256]} | slice | bytes 1572864 | tf_op jit(solution)/shard_map/slice | solution.py:88
  42.4 1.7 %collective-permute-start.16 = (bf16[3,1024,128]{2,1,0:T(8,128)(2,1)S(1)}, bf16[3,1024,128]{2,1,0:T(8,128)(2,1)S(1)}, u32[]{:S(2)}, u32[]{:S(2)}) collective-permute-start(bf16[3,1024,128]{2,1,0:T(8,128)(2,1)S(1)} %slice.69), channel_id=1, source_target_pairs={{0,192},{64,0},{128,64},{192,128},{1,193},{65,1},{129,65},{193,129... | collective-permute-start | bytes 2359304 | tf_op jit(solution)/shard_map/ppermute | solution.py:13
  44.1 1.2 %constant_dynamic-update-slice_fusion.5 = bf16[3,1024,1024]{2,1,0:T(8,128)(2,1)S(1)} fusion(bf16[3,1024,1024]{2,1,0:T(8,128)(2,1)S(1)} %constant_dynamic-update-slice_fusion.6, bf16[3,128,1024]{2,1,0:T(8,128)(2,1)} %collective-permute-done.2), kind=kLoop, calls=%fused_computation.75 | loop fusion | bytes 1572864
  45.5 6.9 %fusion = f32[1024,768,1]{1,0,2:T(8,128)S(1)} fusion(bf16[3,1024,1024]{2,1,0:T(8,128)(2,1)S(1)} %constant_dynamic-update-slice_fusion, bf16[3,1024,256]{2,1,0:T(8,128)(2,1)} %collective-permute-done.9, bf16[3,1024,256]{2,1,0:T(8,128)(2,1)} %collective-permute-done.8, bf16[3,1024,256]{2,1,0:T(8,128)(2,1)S(1)} %copy-done.4), kind=kOutput, calls=%fused_computation | convolution fusion | flops 4845993984 | bytes 14155776 | tf_op jit(solution)/shard_map/lnk,lkc->nc/dot_general | solution.py:106
  52.6 6.9 %collective-permute-start.10 = (bf16[2,128,768]{2,1,0:T(8,128)(2,1)S(1)}, bf16[2,128,768]{2,1,0:T(8,128)(2,1)S(1)}, u32[]{:S(2)}, u32[]{:S(2)}) collective-permute-start(bf16[2,128,768]{2,1,0:T(8,128)(2,1)S(1)} %pad_maximum_fusion.1), channel_id=1, source_target_pairs={{0,1},{1,2},{2,3},{3,4},{4,5},{5,6},{6,7},{7,0},{8,15},{9,8},{10,9... | collective-permute-start | bytes 1179656 | tf_op jit(solution)/shard_map/ppermute | solution.py:40
  59.6 1.2 %collective-permute-start.12 = (bf16[128,768]{1,0:T(8,128)(2,1)S(1)}, bf16[128,768]{1,0:T(8,128)(2,1)S(1)}, u32[]{:S(2)}, u32[]{:S(2)}) collective-permute-start(bf16[128,768]{1,0:T(8,128)(2,1)S(1)} %get-tuple-element.7), channel_id=1, source_target_pairs={{0,2},{1,3},{2,4},{3,5},{4,6},{5,7},{6,0},{7,1},{8,14},{9,15},{10,... | collective-permute-start | bytes 589832 | tf_op jit(solution)/shard_map/ppermute | solution.py:40
  60.8 0.8 collective-permute-start.11
  61.6 1.8 %fusion.6 = f32[1024,256,1]{1,0,2:T(8,128)S(1)} fusion(bf16[3,1024,1024]{2,1,0:T(8,128)(2,1)S(1)} %constant_dynamic-update-slice_fusion, bf16[3,1024,128]{2,1,0:T(8,128)(2,1)S(1)} %collective-permute-done.16, bf16[3,1024,128]{2,1,0:T(8,128)(2,1)S(1)} %collective-permute-done.15), kind=kOutput, calls=%fused_computation.6 | convolution fusion | flops 1613758464 | bytes 8912896 | tf_op jit(solution)/shard_map/lnk,lkc->nc/dot_general | solution.py:106
  63.5 0.8 collective-permute-start.17
  64.3 2.2 %collective-permute-start.19 = (bf16[128,256]{1,0:T(8,128)(2,1)S(1)}, bf16[128,256]{1,0:T(8,128)(2,1)S(1)}, u32[]{:S(2)}, u32[]{:S(2)}) collective-permute-start(bf16[128,256]{1,0:T(8,128)(2,1)S(1)} %get-tuple-element.12), channel_id=1, source_target_pairs={{0,6},{1,7},{2,0},{3,1},{4,2},{5,3},{6,4},{7,5},{8,10},{9,11},{10,... | collective-permute-start | bytes 196616 | tf_op jit(solution)/shard_map/ppermute | solution.py:40
  66.5 1.6 %collective-permute-done.10 = bf16[2,128,768]{2,1,0:T(8,128)(2,1)S(1)} collective-permute-done((bf16[2,128,768]{2,1,0:T(8,128)(2,1)S(1)}, bf16[2,128,768]{2,1,0:T(8,128)(2,1)S(1)}, u32[]{:S(2)}, u32[]{:S(2)}) %collective-permute-start.10) | collective-permute-done | bytes 393248 | tf_op jit(solution)/shard_map/ppermute | solution.py:40
  68.1 3.4 %collective-permute-start.18 = (bf16[2,128,256]{2,1,0:T(8,128)(2,1)S(1)}, bf16[2,128,256]{2,1,0:T(8,128)(2,1)S(1)}, u32[]{:S(2)}, u32[]{:S(2)}) collective-permute-start(bf16[2,128,256]{2,1,0:T(8,128)(2,1)S(1)} %pad_maximum_fusion.4), channel_id=1, source_target_pairs={{0,1},{1,2},{2,3},{3,4},{4,5},{5,6},{6,7},{7,0},{8,15},{9,8},{10,9... | collective-permute-start | bytes 393224 | tf_op jit(solution)/shard_map/ppermute | solution.py:40
  71.6 0.7 collective-permute-done.12
  72.4 4.1 %collective-permute-start.13 = (bf16[128,768]{1,0:T(8,128)(2,1)S(1)}, bf16[128,768]{1,0:T(8,128)(2,1)S(1)}, u32[]{:S(2)}, u32[]{:S(2)}) collective-permute-start(bf16[128,768]{1,0:T(8,128)(2,1)S(1)} %fusion.14), channel_id=1, source_target_pairs={{0,2},{1,3},{2,4},{3,5},{4,6},{5,7},{6,0},{7,1},{8,14},{9,15},{10,... | collective-permute-start | bytes 589832 | tf_op jit(solution)/shard_map/ppermute | solution.py:40
  76.7 0.5 collective-permute-done.17
  77.2 0.7 collective-permute-done.19
  77.9 0.5 collective-permute-start.20
  78.4 3.5 %collective-permute-start.21 = (bf16[128,256]{1,0:T(8,128)(2,1)S(1)}, bf16[128,256]{1,0:T(8,128)(2,1)S(1)}, u32[]{:S(2)}, u32[]{:S(2)}) collective-permute-start(bf16[128,256]{1,0:T(8,128)(2,1)S(1)} %fusion.36), channel_id=1, source_target_pairs={{0,2},{1,3},{2,4},{3,5},{4,6},{5,7},{6,0},{7,1},{8,14},{9,15},{10,... | collective-permute-start | bytes 196616 | tf_op jit(solution)/shard_map/ppermute | solution.py:40
  81.9 3.6 %collective-permute-done.14 = bf16[128,768]{1,0:T(8,128)(2,1)S(1)} collective-permute-done((bf16[128,768]{1,0:T(8,128)(2,1)S(1)}, bf16[128,768]{1,0:T(8,128)(2,1)S(1)}, u32[]{:S(2)}, u32[]{:S(2)}) %collective-permute-start.14) | collective-permute-done | bytes 196640 | tf_op jit(solution)/shard_map/ppermute | solution.py:40
  85.6 2.6 %collective-permute-done.20 = bf16[128,256]{1,0:T(8,128)(2,1)S(1)} collective-permute-done((bf16[128,256]{1,0:T(8,128)(2,1)S(1)}, bf16[128,256]{1,0:T(8,128)(2,1)S(1)}, u32[]{:S(2)}, u32[]{:S(2)}) %collective-permute-start.20) | collective-permute-done | bytes 65568 | tf_op jit(solution)/shard_map/ppermute | solution.py:40
  88.4 0.4 convolution_convert_fusion
  88.8 1.5 %copy.14 = bf16[32,3,4,1024]{3,2,1,0:T(4,128)(2,1)} copy(bf16[32,3,4,1024]{3,0,2,1:T(8,128)(2,1)S(1)} %bitcast.62) | data formatting | bytes 1572864 | tf_op jit(solution)/shard_map/reshape | solution.py:120
  90.2 8.5 %all-to-all-start = ((bf16[32,3,4,1024]{3,2,1,0:T(4,128)(2,1)}), bf16[32,3,4,1024]{3,2,1,0:T(4,128)(2,1)S(1)}, u32[]{:S(2)}, u32[]{:S(2)}) async-start(bf16[32,3,4,1024]{3,2,1,0:T(4,128)(2,1)} %copy.14), calls=%async_computation | async-start | bytes 1572864 | tf_op jit(solution)/shard_map/all_to_all | solution.py:121
  98.7 14.2 %all-to-all-done = bf16[32,3,4,1024]{3,2,1,0:T(4,128)(2,1)S(1)} async-done(((bf16[32,3,4,1024]{3,2,1,0:T(4,128)(2,1)}), bf16[32,3,4,1024]{3,2,1,0:T(4,128)(2,1)S(1)}, u32[]{:S(2)}, u32[]{:S(2)}) %all-to-all-start) | async-done | bytes 786464 | tf_op jit(solution)/shard_map/all_to_all | solution.py:121
  112.9 0.5 multiply_reduce_fusion
  113.7 0.5 fusion.10
  114.4 1.5 %reshape.97 = bf16[1,1,4,12,8192]{4,2,3,1,0:T(4,128)(2,1)} reshape(bf16[4,3,4,8,1024]{4,3,0,2,1:T(8,128)(2,1)S(1)} %copy.17) | data formatting | bytes 1572864 | tf_op jit(solution)/shard_map/reshape | solution.py:129
  (64 shorter events, 2.0 us)
Async XLA Ops:
  0.0 22.7 %copy-start = (s32[4096,1]{0,1:T(1,128)S(1)}, s32[4096,1]{0,1:T(1,128)}, u32[]{:S(2)}) copy-start(s32[4096,1]{0,1:T(1,128)} %param.6) | copy-start | bytes 49156
  0.0 19.1 %collective-permute-start.3 = (bf16[3,128,1024]{2,1,0:T(8,128)(2,1)}, bf16[3,128,1024]{2,1,0:T(8,128)(2,1)S(1)}, u32[]{:S(2)}, u32[]{:S(2)}) collective-permute-start(bf16[3,128,1024]{2,1,0:T(8,128)(2,1)} %bitcast.67), channel_id=1, source_target_pairs={{0,16},{8,24},{16,32},{24,40},{32,48},{40,56},{48,0},{56,8},{1,17}... | collective-permute-start | bytes 2359304 | tf_op jit(solution)/shard_map/ppermute | solution.py:19
  2.1 20.6 %collective-permute-start.1 = (bf16[3,128,1024]{2,1,0:T(8,128)(2,1)}, bf16[3,128,1024]{2,1,0:T(8,128)(2,1)S(1)}, u32[]{:S(2)}, u32[]{:S(2)}) collective-permute-start(bf16[3,128,1024]{2,1,0:T(8,128)(2,1)} %bitcast.68), channel_id=1, source_target_pairs={{0,48},{8,56},{16,0},{24,8},{32,16},{40,24},{48,32},{56,40},{1,49}... | collective-permute-start | bytes 2359304 | tf_op jit(solution)/shard_map/ppermute | solution.py:19
  3.7 34.6 %collective-permute-start.8 = (bf16[3,1024,256]{2,1,0:T(8,128)(2,1)}, bf16[3,1024,256]{2,1,0:T(8,128)(2,1)}, u32[]{:S(2)}, u32[]{:S(2)}) collective-permute-start(bf16[3,1024,256]{2,1,0:T(8,128)(2,1)} %param.5), channel_id=1, source_target_pairs={{0,64},{64,128},{128,192},{192,0},{1,65},{65,129},{129,193},{193,1... | collective-permute-start | bytes 4718600 | tf_op jit(solution)/shard_map/ppermute | solution.py:13
  4.9 36.4 %collective-permute-start.9 = (bf16[3,1024,256]{2,1,0:T(8,128)(2,1)}, bf16[3,1024,256]{2,1,0:T(8,128)(2,1)}, u32[]{:S(2)}, u32[]{:S(2)}) collective-permute-start(bf16[3,1024,256]{2,1,0:T(8,128)(2,1)} %param.5), channel_id=1, source_target_pairs={{0,192},{64,0},{128,64},{192,128},{1,193},{65,1},{129,65},{193,129... | collective-permute-start | bytes 4718600 | tf_op jit(solution)/shard_map/ppermute | solution.py:13
  19.1 9.9 %collective-permute-start.4 = (bf16[3,64,1024]{2,1,0:T(8,128)(2,1)S(1)}, bf16[3,64,1024]{2,1,0:T(8,128)(2,1)S(1)}, u32[]{:S(2)}, u32[]{:S(2)}) collective-permute-start(bf16[3,64,1024]{2,1,0:T(8,128)(2,1)S(1)} %slice.60), channel_id=1, source_target_pairs={{0,16},{8,24},{16,32},{24,40},{32,48},{40,56},{48,0},{56,8},{1,17}... | collective-permute-start | bytes 1179656 | tf_op jit(solution)/shard_map/ppermute | solution.py:19
  20.8 16.3 %collective-permute-start = (bf16[3,128,1024]{2,1,0:T(8,128)(2,1)}, bf16[3,128,1024]{2,1,0:T(8,128)(2,1)S(1)}, u32[]{:S(2)}, u32[]{:S(2)}) collective-permute-start(bf16[3,128,1024]{2,1,0:T(8,128)(2,1)} %bitcast.69), channel_id=1, source_target_pairs={{0,8},{8,0},{16,24},{24,16},{32,40},{40,32},{48,56},{56,48},{1,9},... | collective-permute-start | bytes 2359304 | tf_op jit(solution)/shard_map/ppermute | solution.py:19
  23.5 11.9 %collective-permute-start.5 = (bf16[3,64,1024]{2,1,0:T(8,128)(2,1)}, bf16[3,64,1024]{2,1,0:T(8,128)(2,1)S(1)}, u32[]{:S(2)}, u32[]{:S(2)}) collective-permute-start(bf16[3,64,1024]{2,1,0:T(8,128)(2,1)} %slice.61), channel_id=1, source_target_pairs={{0,48},{8,56},{16,0},{24,8},{32,16},{40,24},{48,32},{56,40},{1,49}... | collective-permute-start | bytes 1179656 | tf_op jit(solution)/shard_map/ppermute | solution.py:19
  29.0 15.1 %collective-permute-start.2 = (bf16[3,128,1024]{2,1,0:T(8,128)(2,1)S(1)}, bf16[3,128,1024]{2,1,0:T(8,128)(2,1)}, u32[]{:S(2)}, u32[]{:S(2)}) collective-permute-start(bf16[3,128,1024]{2,1,0:T(8,128)(2,1)S(1)} %collective-permute-done.1), channel_id=1, source_target_pairs={{0,8},{8,0},{16,24},{24,16},{32,40},{40,32},{48,56},{56,48},{1,9},... | collective-permute-start | bytes 2359304 | tf_op jit(solution)/shard_map/ppermute | solution.py:19
  35.4 9.9 %collective-permute-start.6 = (bf16[3,128,1024]{2,1,0:T(8,128)(2,1)S(1)}, bf16[3,128,1024]{2,1,0:T(8,128)(2,1)S(1)}, u32[]{:S(2)}, u32[]{:S(2)}) collective-permute-start(bf16[3,128,1024]{2,1,0:T(8,128)(2,1)S(1)} %pad_maximum_fusion), channel_id=1, source_target_pairs={{0,8},{8,0},{16,24},{24,16},{32,40},{40,32},{48,56},{56,48},{1,9},... | collective-permute-start | bytes 2359304 | tf_op jit(solution)/shard_map/ppermute | solution.py:19
  37.1 8.4 %collective-permute-start.7 = (bf16[3,128,1024]{2,1,0:T(8,128)(2,1)S(1)}, bf16[3,128,1024]{2,1,0:T(8,128)(2,1)S(1)}, u32[]{:S(2)}, u32[]{:S(2)}) collective-permute-start(bf16[3,128,1024]{2,1,0:T(8,128)(2,1)S(1)} %collective-permute-done.3), channel_id=1, source_target_pairs={{0,8},{8,0},{16,24},{24,16},{32,40},{40,32},{48,56},{56,48},{1,9},... | collective-permute-start | bytes 2359304 | tf_op jit(solution)/shard_map/ppermute | solution.py:19
  37.4 8.2 %copy-start.4 = (bf16[3,1024,256]{2,1,0:T(8,128)(2,1)S(1)}, bf16[3,1024,256]{2,1,0:T(8,128)(2,1)}, u32[]{:S(2)}) copy-start(bf16[3,1024,256]{2,1,0:T(8,128)(2,1)} %param.5) | copy-start | bytes 4718596
  39.4 22.2 %collective-permute-start.15 = (bf16[3,1024,128]{2,1,0:T(8,128)(2,1)S(1)}, bf16[3,1024,128]{2,1,0:T(8,128)(2,1)S(1)}, u32[]{:S(2)}, u32[]{:S(2)}) collective-permute-start(bf16[3,1024,128]{2,1,0:T(8,128)(2,1)S(1)} %slice.68), channel_id=1, source_target_pairs={{0,64},{64,128},{128,192},{192,0},{1,65},{65,129},{129,193},{193,1... | collective-permute-start | bytes 2359304 | tf_op jit(solution)/shard_map/ppermute | solution.py:13
  42.4 19.2 %collective-permute-start.16 = (bf16[3,1024,128]{2,1,0:T(8,128)(2,1)S(1)}, bf16[3,1024,128]{2,1,0:T(8,128)(2,1)S(1)}, u32[]{:S(2)}, u32[]{:S(2)}) collective-permute-start(bf16[3,1024,128]{2,1,0:T(8,128)(2,1)S(1)} %slice.69), channel_id=1, source_target_pairs={{0,192},{64,0},{128,64},{192,128},{1,193},{65,1},{129,65},{193,129... | collective-permute-start | bytes 2359304 | tf_op jit(solution)/shard_map/ppermute | solution.py:13
  52.6 15.5 %collective-permute-start.10 = (bf16[2,128,768]{2,1,0:T(8,128)(2,1)S(1)}, bf16[2,128,768]{2,1,0:T(8,128)(2,1)S(1)}, u32[]{:S(2)}, u32[]{:S(2)}) collective-permute-start(bf16[2,128,768]{2,1,0:T(8,128)(2,1)S(1)} %pad_maximum_fusion.1), channel_id=1, source_target_pairs={{0,1},{1,2},{2,3},{3,4},{4,5},{5,6},{6,7},{7,0},{8,15},{9,8},{10,9... | collective-permute-start | bytes 1179656 | tf_op jit(solution)/shard_map/ppermute | solution.py:40
  59.6 12.8 %collective-permute-start.12 = (bf16[128,768]{1,0:T(8,128)(2,1)S(1)}, bf16[128,768]{1,0:T(8,128)(2,1)S(1)}, u32[]{:S(2)}, u32[]{:S(2)}) collective-permute-start(bf16[128,768]{1,0:T(8,128)(2,1)S(1)} %get-tuple-element.7), channel_id=1, source_target_pairs={{0,2},{1,3},{2,4},{3,5},{4,6},{5,7},{6,0},{7,1},{8,14},{9,15},{10,... | collective-permute-start | bytes 589832 | tf_op jit(solution)/shard_map/ppermute | solution.py:40
  60.8 15.7 %collective-permute-start.11 = (bf16[2,128,768]{2,1,0:T(8,128)(2,1)S(1)}, bf16[2,128,768]{2,1,0:T(8,128)(2,1)S(1)}, u32[]{:S(2)}, u32[]{:S(2)}) collective-permute-start(bf16[2,128,768]{2,1,0:T(8,128)(2,1)S(1)} %pad_maximum_fusion.2), channel_id=1, source_target_pairs={{0,7},{1,0},{2,1},{3,2},{4,3},{5,4},{6,5},{7,6},{8,9},{9,10},{10,1... | collective-permute-start | bytes 1179656 | tf_op jit(solution)/shard_map/ppermute | solution.py:40
  63.4 25.0 %copy-start.1 = (s32[128,32]{0,1:T(8,128)S(1)}, s32[128,32]{0,1:T(8,128)}, u32[]{:S(2)}) copy-start(s32[128,32]{0,1:T(8,128)} %copy.12) | copy-start | bytes 49156
  63.4 25.0 %copy-start.3 = (pred[128,32]{0,1:T(8,128)(4,1)S(1)}, pred[128,32]{0,1:T(8,128)(4,1)}, u32[]{:S(2)}) copy-start(pred[128,32]{0,1:T(8,128)(4,1)} %copy.13) | copy-start | bytes 12292
  63.5 13.7 %collective-permute-start.17 = (bf16[2,128,256]{2,1,0:T(8,128)(2,1)S(1)}, bf16[2,128,256]{2,1,0:T(8,128)(2,1)S(1)}, u32[]{:S(2)}, u32[]{:S(2)}) collective-permute-start(bf16[2,128,256]{2,1,0:T(8,128)(2,1)S(1)} %pad_maximum_fusion.3), channel_id=1, source_target_pairs={{0,7},{1,0},{2,1},{3,2},{4,3},{5,4},{6,5},{7,6},{8,9},{9,10},{10,1... | collective-permute-start | bytes 393224 | tf_op jit(solution)/shard_map/ppermute | solution.py:40
  64.3 13.6 %collective-permute-start.19 = (bf16[128,256]{1,0:T(8,128)(2,1)S(1)}, bf16[128,256]{1,0:T(8,128)(2,1)S(1)}, u32[]{:S(2)}, u32[]{:S(2)}) collective-permute-start(bf16[128,256]{1,0:T(8,128)(2,1)S(1)} %get-tuple-element.12), channel_id=1, source_target_pairs={{0,6},{1,7},{2,0},{3,1},{4,2},{5,3},{6,4},{7,5},{8,10},{9,11},{10,... | collective-permute-start | bytes 196616 | tf_op jit(solution)/shard_map/ppermute | solution.py:40
  68.1 10.3 %collective-permute-start.18 = (bf16[2,128,256]{2,1,0:T(8,128)(2,1)S(1)}, bf16[2,128,256]{2,1,0:T(8,128)(2,1)S(1)}, u32[]{:S(2)}, u32[]{:S(2)}) collective-permute-start(bf16[2,128,256]{2,1,0:T(8,128)(2,1)S(1)} %pad_maximum_fusion.4), channel_id=1, source_target_pairs={{0,1},{1,2},{2,3},{3,4},{4,5},{5,6},{6,7},{7,0},{8,15},{9,8},{10,9... | collective-permute-start | bytes 393224 | tf_op jit(solution)/shard_map/ppermute | solution.py:40
  71.6 27.1 %copy-start.2 = (f32[8192]{0:T(1024)S(1)}, f32[8192]{0:T(1024)}, u32[]{:S(2)}) copy-start(f32[8192]{0:T(1024)} %param.7) | copy-start | bytes 98308
  72.4 9.5 %collective-permute-start.13 = (bf16[128,768]{1,0:T(8,128)(2,1)S(1)}, bf16[128,768]{1,0:T(8,128)(2,1)S(1)}, u32[]{:S(2)}, u32[]{:S(2)}) collective-permute-start(bf16[128,768]{1,0:T(8,128)(2,1)S(1)} %fusion.14), channel_id=1, source_target_pairs={{0,2},{1,3},{2,4},{3,5},{4,6},{5,7},{6,0},{7,1},{8,14},{9,15},{10,... | collective-permute-start | bytes 589832 | tf_op jit(solution)/shard_map/ppermute | solution.py:40
  76.6 8.9 %collective-permute-start.14 = (bf16[128,768]{1,0:T(8,128)(2,1)S(1)}, bf16[128,768]{1,0:T(8,128)(2,1)S(1)}, u32[]{:S(2)}, u32[]{:S(2)}) collective-permute-start(bf16[128,768]{1,0:T(8,128)(2,1)S(1)} %fusion.22), channel_id=1, source_target_pairs={{0,6},{1,7},{2,0},{3,1},{4,2},{5,3},{6,4},{7,5},{8,10},{9,11},{10,... | collective-permute-start | bytes 589832 | tf_op jit(solution)/shard_map/ppermute | solution.py:40
  77.9 10.3 %collective-permute-start.20 = (bf16[128,256]{1,0:T(8,128)(2,1)S(1)}, bf16[128,256]{1,0:T(8,128)(2,1)S(1)}, u32[]{:S(2)}, u32[]{:S(2)}) collective-permute-start(bf16[128,256]{1,0:T(8,128)(2,1)S(1)} %fusion.28), channel_id=1, source_target_pairs={{0,6},{1,7},{2,0},{3,1},{4,2},{5,3},{6,4},{7,5},{8,10},{9,11},{10,... | collective-permute-start | bytes 196616 | tf_op jit(solution)/shard_map/ppermute | solution.py:40
  78.4 9.8 %collective-permute-start.21 = (bf16[128,256]{1,0:T(8,128)(2,1)S(1)}, bf16[128,256]{1,0:T(8,128)(2,1)S(1)}, u32[]{:S(2)}, u32[]{:S(2)}) collective-permute-start(bf16[128,256]{1,0:T(8,128)(2,1)S(1)} %fusion.36), channel_id=1, source_target_pairs={{0,2},{1,3},{2,4},{3,5},{4,6},{5,7},{6,0},{7,1},{8,14},{9,15},{10,... | collective-permute-start | bytes 196616 | tf_op jit(solution)/shard_map/ppermute | solution.py:40
  90.2 22.7 %all-to-all-start = ((bf16[32,3,4,1024]{3,2,1,0:T(4,128)(2,1)}), bf16[32,3,4,1024]{3,2,1,0:T(4,128)(2,1)S(1)}, u32[]{:S(2)}, u32[]{:S(2)}) async-start(bf16[32,3,4,1024]{3,2,1,0:T(4,128)(2,1)} %copy.14), calls=%async_computation | async-start | bytes 1572864 | tf_op jit(solution)/shard_map/all_to_all | solution.py:121

commit v4 on v3

--- a/solution.py
+++ b/solution.py
@@ -58,6 +58,20 @@
     return total.astype(BF16)
 
 
+def relay(up, down, core, axes):
+    n_s, n_b = lax.axis_size("section"), lax.axis_size("batch")
+    pairs = []
+    for s in range(n_s):
+        for b in range(n_b):
+            step = 1 if b % 2 == 0 else -1
+            if axes == "section":
+                to = ((s + step) % n_s) * n_b + b
+            else:
+                to = s * n_b + ((b // 2 + step) % (n_b // 2)) * 2 + b % 2
+            pairs.append((s * n_b + b, to))
+    return lax.ppermute(jnp.where(core == 0, up, down), ("section", "batch"), pairs)
+
+
 def body(captured, fc_weight, owner, norm_gain):
     n_section = lax.axis_size("section")
     n_batch = lax.axis_size("batch")
@@ -73,20 +87,15 @@
     yi, ci = bi // 2, bi % 2
 
     own = captured.transpose(1, 0, 2)
-    half = col // 2
     w_up = shift(fc_weight, "section", 1)
     w_dn = shift(fc_weight, "section", -1)
     y_up = hop(own, 1, 0)
     y_dn = hop(own, -1, 0)
     sib = hop(own, 0, 1)
-    r2 = rows // 2
-    far_top = hop(y_up[:, :r2], 1, 0)
-    far_bot = hop(y_dn[:, r2:], -1, 0)
+    y_far = relay(y_up, y_dn, ci, "batch")
     y_up_s = hop(y_up, 0, 1)
     y_dn_s = hop(y_dn, 0, 1)
-    far_a = shift(w_up[:, :, :half], "section", 1)
-    far_b = shift(w_dn[:, :, half:], "section", -1)
-    y_far = jnp.concatenate([far_top, far_bot], axis=1)
+    w_far = relay(w_up, w_dn, ci, "section")
     y_far_s = hop(y_far, 0, 1)
     tokens = jnp.concatenate(
         [own, sib, y_dn, y_dn_s, y_far, y_far_s, y_up, y_up_s], axis=1
@@ -108,7 +117,7 @@
         return reduce_z(part, place, sign)
 
     first = job([fc_weight, w_up, w_dn], 1)
-    second = job([far_a, far_b], -1)
+    second = job([w_far], -1)
     done = [first, second]
     here = jnp.concatenate(
         [first[:, :col], first[:, 2 * col :], second, first[:, col : 2 * col]], axis=1

time: 116 us -> 146 us (1.26)
  waiting for transfers between devices: 38 us -> 65.4 us
  starting transfers between devices: 52.1 us -> 43.1 us
  matrix products: 9.06 us -> 13.6 us
  other arithmetic: 4.8 us -> 9 us
  local copies, waits for them, and re-layouts: 11.6 us -> 13.6 us
    ppermute x10, waiting for transfers between devices: 9.69 us -> 25 us  [mirror(): return lax.ppermute(value, ('batch', 'tensor'), pairs)]
    ppermute x0 -> x2, waiting for transfers between devices: none -> 8.93 us  [relay(): lax.ppermute(jnp.where(core == 0, up, down), ('section', 'batch'), pairs)]
    ppermute x10, starting transfers between devices: 23.5 us -> 16.8 us  [mirror(): return lax.ppermute(value, ('batch', 'tensor'), pairs)]
    unnamed x25 -> x23, local copies, waits for them, and re-layouts: 2.81 us -> 9.05 us
    ppermute x8 -> x6, starting transfers between devices: 14 us -> 8.51 us  [hop(): return lax.ppermute(value, 'batch', pairs)]
    ppermute x0 -> x2, starting transfers between devices: none -> 5 us  [relay(): lax.ppermute(jnp.where(core == 0, up, down), ('section', 'batch'), pairs)]
    dot_general x2, matrix products: 8.7 us -> 13.3 us  [job(): part = jnp.einsum('lnk,lkc->nc', tokens, weight, preferred_element_type=F32)]
    select_n x0 -> x2, other arithmetic: none -> 4.22 us  [relay(): jnp.where(core == 0, up, down)]
  transfers between devices with their start and end apart: 23 -> 21, of which waited for: 10 -> 11; matrix products, arithmetic and copies ran while one was open for 18% -> 17% of each run, Pallas kernels for 0% -> 0%
where the time goes in v4:
time: 146 us; the launch traced here: 145 us
  waiting for transfers between devices  65.4 us (45%)
  starting transfers between devices  43.1 us (30%)
  local copies, waits for them, and re-layouts  13.6 us (9%)
  matrix products  13.6 us (9%)
  other arithmetic  9 us (6%)
    ppermute x10, waiting for transfers between devices, mirror(): return lax.ppermute(value, ('batch', 'tensor'), pairs)  25 us
    ppermute x10, starting transfers between devices, mirror(): return lax.ppermute(value, ('batch', 'tensor'), pairs)  16.8 us
    all_to_all x1, waiting for transfers between devices, body(): lax.all_to_all(outgoing, ('section', 'batch'), split_axis=0, concat_axis=...  14.2 us
    ppermute x6, waiting for transfers between devices, hop(): return lax.ppermute(value, 'batch', pairs)  14 us
    dot_general x2, matrix products, job(): part = jnp.einsum('lnk,lkc->nc', tokens, weight, preferred_element_type=F32)  13.3 us
    all_to_all x1, starting transfers between devices, body(): lax.all_to_all(outgoing, ('section', 'batch'), split_axis=0, concat_axis=...  10.1 us
    unnamed x23, local copies, waits for them, and re-layouts  9.05 us
    ppermute x2, waiting for transfers between devices, relay(): lax.ppermute(jnp.where(core == 0, up, down), ('section', 'batch'), pairs)  8.93 us
  transfers between devices with their start and end apart: 21, of which 11 were waited for; matrix products, arithmetic and copies ran while one was open for 17% of the time, Pallas kernels for 0%

profile of v4, /device:TPU:1, one launch (start us, length us, event | category | flops | bytes accessed | tf_op | source)
XLA Modules:
  0.0 145.0 jit_solution(15454676100059086081)
XLA Ops:
  0.0 3.2 %collective-permute-start = (bf16[3,128,1024]{2,1,0:T(8,128)(2,1)}, bf16[3,128,1024]{2,1,0:T(8,128)(2,1)S(1)}, u32[]{:S(2)}, u32[]{:S(2)}) collective-permute-start(bf16[3,128,1024]{2,1,0:T(8,128)(2,1)} %bitcast.68), channel_id=1, source_target_pairs={{0,8},{8,0},{16,24},{24,16},{32,40},{40,32},{48,56},{56,48},{1,9},... | collective-permute-start | bytes 2359304 | tf_op jit(solution)/shard_map/ppermute | solution.py:19
  3.2 2.7 %collective-permute-start.1 = (bf16[3,128,1024]{2,1,0:T(8,128)(2,1)}, bf16[3,128,1024]{2,1,0:T(8,128)(2,1)}, u32[]{:S(2)}, u32[]{:S(2)}) collective-permute-start(bf16[3,128,1024]{2,1,0:T(8,128)(2,1)} %bitcast.70), channel_id=1, source_target_pairs={{0,48},{8,56},{16,0},{24,8},{32,16},{40,24},{48,32},{56,40},{1,49}... | collective-permute-start | bytes 2359304 | tf_op jit(solution)/shard_map/ppermute | solution.py:19
  5.9 2.7 %collective-permute-start.8 = (bf16[3,1024,256]{2,1,0:T(8,128)(2,1)}, bf16[3,1024,256]{2,1,0:T(8,128)(2,1)}, u32[]{:S(2)}, u32[]{:S(2)}) collective-permute-start(bf16[3,1024,256]{2,1,0:T(8,128)(2,1)} %param.5), channel_id=1, source_target_pairs={{0,192},{64,0},{128,64},{192,128},{1,193},{65,1},{129,65},{193,129... | collective-permute-start | bytes 4718600 | tf_op jit(solution)/shard_map/ppermute | solution.py:13
  8.6 1.2 constant_dynamic-update-slice_fusion.7
  9.9 14.0 %collective-permute-done.3 = bf16[3,128,1024]{2,1,0:T(8,128)(2,1)S(1)} collective-permute-done((bf16[3,128,1024]{2,1,0:T(8,128)(2,1)}, bf16[3,128,1024]{2,1,0:T(8,128)(2,1)S(1)}, u32[]{:S(2)}, u32[]{:S(2)}) %collective-permute-start.3) | collective-permute-done | bytes 786464 | tf_op jit(solution)/shard_map/ppermute | solution.py:19
  23.8 1.5 %broadcast_select_fusion.1 = (bf16[3,128,1024]{2,1,0:T(8,128)(2,1)S(1)}, bf16[3,1024,1024]{2,1,0:T(8,128)(2,1)S(1)}) fusion(bf16[3,128,1024]{2,1,0:T(8,128)(2,1)S(1)} %collective-permute-done.3, bf16[3,128,1024]{2,1,0:T(8,128)(2,1)} %collective-permute-done.1, pred[]{:T(512)S(6)} %eq.111, bf16[3,1024,1024]{2,1,0:T(8,128)(2,1)S(1)} %constant_dynamic-update-slice_fusion.6), kind=kLoop, calls=%fused_computation.11 | loop fusion | flops 393216 | bytes 3145729 | tf_op jit(solution)/shard_map/jit(_where)/select_n | solution.py:72
  25.4 2.5 %collective-permute-start.4 = (bf16[3,128,1024]{2,1,0:T(8,128)(2,1)S(1)}, bf16[3,128,1024]{2,1,0:T(8,128)(2,1)S(1)}, u32[]{:S(2)}, u32[]{:S(2)}) collective-permute-start(bf16[3,128,1024]{2,1,0:T(8,128)(2,1)S(1)} %get-tuple-element.17), channel_id=1, source_target_pairs={{0,16},{8,56},{16,32},{24,8},{32,48},{40,24},{48,0},{56,40},{64,80... | collective-permute-start | bytes 2359304 | tf_op jit(solution)/shard_map/ppermute | solution.py:72
  27.9 8.9 %collective-permute-done.4 = bf16[3,128,1024]{2,1,0:T(8,128)(2,1)S(1)} collective-permute-done((bf16[3,128,1024]{2,1,0:T(8,128)(2,1)S(1)}, bf16[3,128,1024]{2,1,0:T(8,128)(2,1)S(1)}, u32[]{:S(2)}, u32[]{:S(2)}) %collective-permute-start.4) | collective-permute-done | bytes 786464 | tf_op jit(solution)/shard_map/ppermute | solution.py:72
  36.8 2.6 %collective-permute-start.5 = (bf16[3,128,1024]{2,1,0:T(8,128)(2,1)S(1)}, bf16[3,128,1024]{2,1,0:T(8,128)(2,1)}, u32[]{:S(2)}, u32[]{:S(2)}) collective-permute-start(bf16[3,128,1024]{2,1,0:T(8,128)(2,1)S(1)} %collective-permute-done.4), channel_id=1, source_target_pairs={{0,8},{8,0},{16,24},{24,16},{32,40},{40,32},{48,56},{56,48},{1,9},... | collective-permute-start | bytes 2359304 | tf_op jit(solution)/shard_map/ppermute | solution.py:19
  39.4 3.3 %collective-permute-done.7 = bf16[3,1024,256]{2,1,0:T(8,128)(2,1)S(1)} collective-permute-done((bf16[3,1024,256]{2,1,0:T(8,128)(2,1)}, bf16[3,1024,256]{2,1,0:T(8,128)(2,1)S(1)}, u32[]{:S(2)}, u32[]{:S(2)}) %collective-permute-start.7) | collective-permute-done | bytes 1572896 | tf_op jit(solution)/shard_map/ppermute | solution.py:13
  42.7 2.7 %broadcast_select_fusion = bf16[3,1024,256]{2,1,0:T(8,128)(2,1)} fusion(bf16[3,1024,256]{2,1,0:T(8,128)(2,1)S(1)} %collective-permute-done.7, bf16[3,1024,256]{2,1,0:T(8,128)(2,1)} %collective-permute-done.8, pred[]{:T(512)S(6)} %eq.111), kind=kLoop, calls=%fused_computation.8 | loop fusion | flops 786432 | bytes 4718593 | tf_op jit(solution)/shard_map/jit(_where)/select_n | solution.py:72
  45.4 2.5 %collective-permute-start.14 = (bf16[3,1024,256]{2,1,0:T(8,128)(2,1)}, bf16[3,1024,256]{2,1,0:T(8,128)(2,1)}, u32[]{:S(2)}, u32[]{:S(2)}) collective-permute-start(bf16[3,1024,256]{2,1,0:T(8,128)(2,1)} %broadcast_select_fusion), channel_id=1, source_target_pairs={{0,64},{8,200},{16,80},{24,216},{32,96},{40,232},{48,112},{56,248}... | collective-permute-start | bytes 4718600 | tf_op jit(solution)/shard_map/ppermute | solution.py:72
  47.9 2.1 %constant_dynamic-update-slice_fusion.4 = bf16[3,1024,1024]{2,1,0:T(8,128)(2,1)} fusion(bf16[3,1024,1024]{2,1,0:T(8,128)(2,1)} %copy-done.2, bf16[3,128,1024]{2,1,0:T(8,128)(2,1)} %collective-permute-done.2), kind=kLoop, calls=%fused_computation.71 | loop fusion | bytes 1572864
  50.0 0.9 constant_dynamic-update-slice_fusion.3
  50.9 2.1 %constant_dynamic-update-slice_fusion.2 = bf16[3,1024,1024]{2,1,0:T(8,128)(2,1)} fusion(bf16[3,1024,1024]{2,1,0:T(8,128)(2,1)} %constant_dynamic-update-slice_fusion.3, bf16[3,128,1024]{2,1,0:T(8,128)(2,1)} %collective-permute-done.5), kind=kLoop, calls=%fused_computation.69 | loop fusion | bytes 1572864
  52.9 0.9 constant_dynamic-update-slice_fusion.1
  53.9 0.9 constant_dynamic-update-slice_fusion
  54.8 8.3 %fusion = f32[1024,768,1]{1,0,2:T(8,128)S(1)} fusion(bf16[3,1024,1024]{2,1,0:T(8,128)(2,1)} %constant_dynamic-update-slice_fusion, bf16[3,1024,256]{2,1,0:T(8,128)(2,1)} %collective-permute-done.8, bf16[3,1024,256]{2,1,0:T(8,128)(2,1)S(1)} %collective-permute-done.7, bf16[3,1024,256]{2,1,0:T(8,128)(2,1)S(1)} %copy-done.4), kind=kOutput, calls=%fused_computation | convolution fusion | flops 4845993984 | bytes 14155776 | tf_op jit(solution)/shard_map/lnk,lkc->nc/dot_general | solution.py:115
  63.1 1.7 %copy-done.1 = f32[1024,768,1]{1,0,2:T(8,128)} copy-done((f32[1024,768,1]{1,0,2:T(8,128)}, f32[1024,768,1]{1,0,2:T(8,128)S(1)}, u32[]{:S(2)}) %copy-start.1) | copy-done | bytes 3145752
  64.8 0.1 fusion.17
  64.9 4.1 %collective-permute-start.9 = (bf16[2,128,768]{2,1,0:T(8,128)(2,1)S(1)}, bf16[2,128,768]{2,1,0:T(8,128)(2,1)S(1)}, u32[]{:S(2)}, u32[]{:S(2)}) collective-permute-start(bf16[2,128,768]{2,1,0:T(8,128)(2,1)S(1)} %pad_maximum_fusion), channel_id=1, source_target_pairs={{0,1},{1,2},{2,3},{3,4},{4,5},{5,6},{6,7},{7,0},{8,15},{9,8},{10,9... | collective-permute-start | bytes 1179656 | tf_op jit(solution)/shard_map/ppermute | solution.py:40
  69.1 1.2 collective-permute-start.11
  70.4 0.8 collective-permute-start.10
  71.3 0.2 reduce_window_sum.11
  71.4 8.3 %collective-permute-done.9 = bf16[2,128,768]{2,1,0:T(8,128)(2,1)S(1)} collective-permute-done((bf16[2,128,768]{2,1,0:T(8,128)(2,1)S(1)}, bf16[2,128,768]{2,1,0:T(8,128)(2,1)S(1)}, u32[]{:S(2)}, u32[]{:S(2)}) %collective-permute-start.9) | collective-permute-done | bytes 393248 | tf_op jit(solution)/shard_map/ppermute | solution.py:40
  79.8 2.5 %collective-permute-done.11 = bf16[128,768]{1,0:T(8,128)(2,1)S(1)} collective-permute-done((bf16[128,768]{1,0:T(8,128)(2,1)S(1)}, bf16[128,768]{1,0:T(8,128)(2,1)S(1)}, u32[]{:S(2)}, u32[]{:S(2)}) %collective-permute-start.11) | collective-permute-done | bytes 196640 | tf_op jit(solution)/shard_map/ppermute | solution.py:40
  82.2 1.0 fusion.10
  83.3 4.1 %collective-permute-start.12 = (bf16[128,768]{1,0:T(8,128)(2,1)S(1)}, bf16[128,768]{1,0:T(8,128)(2,1)S(1)}, u32[]{:S(2)}, u32[]{:S(2)}) collective-permute-start(bf16[128,768]{1,0:T(8,128)(2,1)S(1)} %fusion.10), channel_id=1, source_target_pairs={{0,2},{1,3},{2,4},{3,5},{4,6},{5,7},{6,0},{7,1},{8,14},{9,15},{10,... | collective-permute-start | bytes 589832 | tf_op jit(solution)/shard_map/ppermute | solution.py:40
  87.4 1.0 fusion.18
  88.6 0.1 copy.13
  88.7 3.1 %collective-permute-done.12 = bf16[128,768]{1,0:T(8,128)(2,1)S(1)} collective-permute-done((bf16[128,768]{1,0:T(8,128)(2,1)S(1)}, bf16[128,768]{1,0:T(8,128)(2,1)S(1)}, u32[]{:S(2)}, u32[]{:S(2)}) %collective-permute-start.12) | collective-permute-done | bytes 196640 | tf_op jit(solution)/shard_map/ppermute | solution.py:40
  91.9 5.8 %collective-permute-done.13 = bf16[128,768]{1,0:T(8,128)(2,1)S(1)} collective-permute-done((bf16[128,768]{1,0:T(8,128)(2,1)S(1)}, bf16[128,768]{1,0:T(8,128)(2,1)S(1)}, u32[]{:S(2)}, u32[]{:S(2)}) %collective-permute-start.13) | collective-permute-done | bytes 196640 | tf_op jit(solution)/shard_map/ppermute | solution.py:40
  97.7 1.1 fusion.14
  98.8 5.0 %fusion.38 = f32[1024,256,1]{1,0,2:T(8,128)S(1)} fusion(bf16[3,1024,1024]{2,1,0:T(8,128)(2,1)} %constant_dynamic-update-slice_fusion, bf16[3,1024,256]{2,1,0:T(8,128)(2,1)} %collective-permute-done.14), kind=kOutput, calls=%fused_computation.84 | convolution fusion | flops 1610612736 | bytes 8912896 | tf_op jit(solution)/shard_map/lnk,lkc->nc/dot_general | solution.py:115
  104.1 2.6 %collective-permute-start.16 = (bf16[2,128,256]{2,1,0:T(8,128)(2,1)S(1)}, bf16[2,128,256]{2,1,0:T(8,128)(2,1)S(1)}, u32[]{:S(2)}, u32[]{:S(2)}) collective-permute-start(bf16[2,128,256]{2,1,0:T(8,128)(2,1)S(1)} %pad_maximum_fusion.3), channel_id=1, source_target_pairs={{0,1},{1,2},{2,3},{3,4},{4,5},{5,6},{6,7},{7,0},{8,15},{9,8},{10,9... | collective-permute-start | bytes 393224 | tf_op jit(solution)/shard_map/ppermute | solution.py:40
  106.8 3.1 %collective-permute-done.15 = bf16[2,128,256]{2,1,0:T(8,128)(2,1)S(1)} collective-permute-done((bf16[2,128,256]{2,1,0:T(8,128)(2,1)S(1)}, bf16[2,128,256]{2,1,0:T(8,128)(2,1)S(1)}, u32[]{:S(2)}, u32[]{:S(2)}) %collective-permute-start.15) | collective-permute-done | bytes 131104 | tf_op jit(solution)/shard_map/ppermute | solution.py:40
  110.1 3.6 %collective-permute-start.19 = (bf16[128,256]{1,0:T(8,128)(2,1)S(1)}, bf16[128,256]{1,0:T(8,128)(2,1)S(1)}, u32[]{:S(2)}, u32[]{:S(2)}) collective-permute-start(bf16[128,256]{1,0:T(8,128)(2,1)S(1)} %fusion.32), channel_id=1, source_target_pairs={{0,2},{1,3},{2,4},{3,5},{4,6},{5,7},{6,0},{7,1},{8,14},{9,15},{10,... | collective-permute-start | bytes 196616 | tf_op jit(solution)/shard_map/ppermute | solution.py:40
  113.7 2.1 %collective-permute-done.18 = bf16[128,256]{1,0:T(8,128)(2,1)S(1)} collective-permute-done((bf16[128,256]{1,0:T(8,128)(2,1)S(1)}, bf16[128,256]{1,0:T(8,128)(2,1)S(1)}, u32[]{:S(2)}, u32[]{:S(2)}) %collective-permute-start.18) | collective-permute-done | bytes 65568 | tf_op jit(solution)/shard_map/ppermute | solution.py:40
  115.9 0.4 convolution_convert_fusion
  116.3 1.5 %copy.14 = bf16[32,3,4,1024]{3,2,1,0:T(4,128)(2,1)} copy(bf16[32,3,4,1024]{3,0,2,1:T(8,128)(2,1)S(1)} %bitcast.63) | data formatting | bytes 1572864 | tf_op jit(solution)/shard_map/reshape | solution.py:129
  117.8 10.1 %all-to-all-start = ((bf16[32,3,4,1024]{3,2,1,0:T(4,128)(2,1)}), bf16[32,3,4,1024]{3,2,1,0:T(4,128)(2,1)S(1)}, u32[]{:S(2)}, u32[]{:S(2)}) async-start(bf16[32,3,4,1024]{3,2,1,0:T(4,128)(2,1)} %copy.14), calls=%async_computation | async-start | bytes 1572864 | tf_op jit(solution)/shard_map/all_to_all | solution.py:130
  127.9 14.2 %all-to-all-done = bf16[32,3,4,1024]{3,2,1,0:T(4,128)(2,1)S(1)} async-done(((bf16[32,3,4,1024]{3,2,1,0:T(4,128)(2,1)}), bf16[32,3,4,1024]{3,2,1,0:T(4,128)(2,1)S(1)}, u32[]{:S(2)}, u32[]{:S(2)}) %all-to-all-start) | async-done | bytes 786464 | tf_op jit(solution)/shard_map/all_to_all | solution.py:130
  142.1 0.5 multiply_reduce_fusion
  142.6 0.1 copy.20
  142.7 0.1 copy.16
  142.8 0.5 fusion.6
  143.3 0.2 copy.17
  143.6 1.5 %reshape.97 = bf16[1,1,4,12,8192]{4,2,3,1,0:T(4,128)(2,1)} reshape(bf16[4,3,4,8,1024]{4,3,0,2,1:T(8,128)(2,1)S(1)} %copy.17) | data formatting | bytes 1572864 | tf_op jit(solution)/shard_map/reshape | solution.py:138
  (55 shorter events, 1.1 us)
Async XLA Ops:
  0.0 69.1 %copy-start = (s32[4096,1]{0,1:T(1,128)S(1)}, s32[4096,1]{0,1:T(1,128)}, u32[]{:S(2)}) copy-start(s32[4096,1]{0,1:T(1,128)} %param.6) | copy-start | bytes 49156
  0.0 9.8 %collective-permute-start = (bf16[3,128,1024]{2,1,0:T(8,128)(2,1)}, bf16[3,128,1024]{2,1,0:T(8,128)(2,1)S(1)}, u32[]{:S(2)}, u32[]{:S(2)}) collective-permute-start(bf16[3,128,1024]{2,1,0:T(8,128)(2,1)} %bitcast.68), channel_id=1, source_target_pairs={{0,8},{8,0},{16,24},{24,16},{32,40},{40,32},{48,56},{56,48},{1,9},... | collective-permute-start | bytes 2359304 | tf_op jit(solution)/shard_map/ppermute | solution.py:19
  3.2 20.6 %collective-permute-start.3 = (bf16[3,128,1024]{2,1,0:T(8,128)(2,1)}, bf16[3,128,1024]{2,1,0:T(8,128)(2,1)S(1)}, u32[]{:S(2)}, u32[]{:S(2)}) collective-permute-start(bf16[3,128,1024]{2,1,0:T(8,128)(2,1)} %bitcast.69), channel_id=1, source_target_pairs={{0,16},{8,24},{16,32},{24,40},{32,48},{40,56},{48,0},{56,8},{1,17}... | collective-permute-start | bytes 2359304 | tf_op jit(solution)/shard_map/ppermute | solution.py:19
  3.2 20.6 %collective-permute-start.1 = (bf16[3,128,1024]{2,1,0:T(8,128)(2,1)}, bf16[3,128,1024]{2,1,0:T(8,128)(2,1)}, u32[]{:S(2)}, u32[]{:S(2)}) collective-permute-start(bf16[3,128,1024]{2,1,0:T(8,128)(2,1)} %bitcast.70), channel_id=1, source_target_pairs={{0,48},{8,56},{16,0},{24,8},{32,16},{40,24},{48,32},{56,40},{1,49}... | collective-permute-start | bytes 2359304 | tf_op jit(solution)/shard_map/ppermute | solution.py:19
  5.9 36.8 %collective-permute-start.7 = (bf16[3,1024,256]{2,1,0:T(8,128)(2,1)}, bf16[3,1024,256]{2,1,0:T(8,128)(2,1)S(1)}, u32[]{:S(2)}, u32[]{:S(2)}) collective-permute-start(bf16[3,1024,256]{2,1,0:T(8,128)(2,1)} %param.5), channel_id=1, source_target_pairs={{0,64},{64,128},{128,192},{192,0},{1,65},{65,129},{129,193},{193,1... | collective-permute-start | bytes 4718600 | tf_op jit(solution)/shard_map/ppermute | solution.py:13
  5.9 36.8 %collective-permute-start.8 = (bf16[3,1024,256]{2,1,0:T(8,128)(2,1)}, bf16[3,1024,256]{2,1,0:T(8,128)(2,1)}, u32[]{:S(2)}, u32[]{:S(2)}) collective-permute-start(bf16[3,1024,256]{2,1,0:T(8,128)(2,1)} %param.5), channel_id=1, source_target_pairs={{0,192},{64,0},{128,64},{192,128},{1,193},{65,1},{129,65},{193,129... | collective-permute-start | bytes 4718600 | tf_op jit(solution)/shard_map/ppermute | solution.py:13
  25.4 11.5 %copy-start.2 = (bf16[3,1024,1024]{2,1,0:T(8,128)(2,1)}, bf16[3,1024,1024]{2,1,0:T(8,128)(2,1)S(1)}, u32[]{:S(2)}) copy-start(bf16[3,1024,1024]{2,1,0:T(8,128)(2,1)S(1)} %get-tuple-element.18) | copy-start | bytes 18874372
  25.4 11.5 %collective-permute-start.4 = (bf16[3,128,1024]{2,1,0:T(8,128)(2,1)S(1)}, bf16[3,128,1024]{2,1,0:T(8,128)(2,1)S(1)}, u32[]{:S(2)}, u32[]{:S(2)}) collective-permute-start(bf16[3,128,1024]{2,1,0:T(8,128)(2,1)S(1)} %get-tuple-element.17), channel_id=1, source_target_pairs={{0,16},{8,56},{16,32},{24,8},{32,48},{40,24},{48,0},{56,40},{64,80... | collective-permute-start | bytes 2359304 | tf_op jit(solution)/shard_map/ppermute | solution.py:72
  27.9 20.0 %collective-permute-start.2 = (bf16[3,128,1024]{2,1,0:T(8,128)(2,1)}, bf16[3,128,1024]{2,1,0:T(8,128)(2,1)}, u32[]{:S(2)}, u32[]{:S(2)}) collective-permute-start(bf16[3,128,1024]{2,1,0:T(8,128)(2,1)} %collective-permute-done.1), channel_id=1, source_target_pairs={{0,8},{8,0},{16,24},{24,16},{32,40},{40,32},{48,56},{56,48},{1,9},... | collective-permute-start | bytes 2359304 | tf_op jit(solution)/shard_map/ppermute | solution.py:19
  36.8 14.0 %collective-permute-start.5 = (bf16[3,128,1024]{2,1,0:T(8,128)(2,1)S(1)}, bf16[3,128,1024]{2,1,0:T(8,128)(2,1)}, u32[]{:S(2)}, u32[]{:S(2)}) collective-permute-start(bf16[3,128,1024]{2,1,0:T(8,128)(2,1)S(1)} %collective-permute-done.4), channel_id=1, source_target_pairs={{0,8},{8,0},{16,24},{24,16},{32,40},{40,32},{48,56},{56,48},{1,9},... | collective-permute-start | bytes 2359304 | tf_op jit(solution)/shard_map/ppermute | solution.py:19
  39.4 14.4 %collective-permute-start.6 = (bf16[3,128,1024]{2,1,0:T(8,128)(2,1)S(1)}, bf16[3,128,1024]{2,1,0:T(8,128)(2,1)S(1)}, u32[]{:S(2)}, u32[]{:S(2)}) collective-permute-start(bf16[3,128,1024]{2,1,0:T(8,128)(2,1)S(1)} %collective-permute-done.3), channel_id=1, source_target_pairs={{0,8},{8,0},{16,24},{24,16},{32,40},{40,32},{48,56},{56,48},{1,9},... | collective-permute-start | bytes 2359304 | tf_op jit(solution)/shard_map/ppermute | solution.py:19
  45.4 9.4 %copy-start.4 = (bf16[3,1024,256]{2,1,0:T(8,128)(2,1)S(1)}, bf16[3,1024,256]{2,1,0:T(8,128)(2,1)}, u32[]{:S(2)}) copy-start(bf16[3,1024,256]{2,1,0:T(8,128)(2,1)} %param.5) | copy-start | bytes 4718596
  45.4 53.3 %collective-permute-start.14 = (bf16[3,1024,256]{2,1,0:T(8,128)(2,1)}, bf16[3,1024,256]{2,1,0:T(8,128)(2,1)}, u32[]{:S(2)}, u32[]{:S(2)}) collective-permute-start(bf16[3,1024,256]{2,1,0:T(8,128)(2,1)} %broadcast_select_fusion), channel_id=1, source_target_pairs={{0,64},{8,200},{16,80},{24,216},{32,96},{40,232},{48,112},{56,248}... | collective-permute-start | bytes 4718600 | tf_op jit(solution)/shard_map/ppermute | solution.py:72
  63.1 1.7 %copy-start.1 = (f32[1024,768,1]{1,0,2:T(8,128)}, f32[1024,768,1]{1,0,2:T(8,128)S(1)}, u32[]{:S(2)}) copy-start(f32[1024,768,1]{1,0,2:T(8,128)S(1)} %fusion) | copy-start | bytes 9437188
  64.9 14.8 %collective-permute-start.9 = (bf16[2,128,768]{2,1,0:T(8,128)(2,1)S(1)}, bf16[2,128,768]{2,1,0:T(8,128)(2,1)S(1)}, u32[]{:S(2)}, u32[]{:S(2)}) collective-permute-start(bf16[2,128,768]{2,1,0:T(8,128)(2,1)S(1)} %pad_maximum_fusion), channel_id=1, source_target_pairs={{0,1},{1,2},{2,3},{3,4},{4,5},{5,6},{6,7},{7,0},{8,15},{9,8},{10,9... | collective-permute-start | bytes 1179656 | tf_op jit(solution)/shard_map/ppermute | solution.py:40
  69.1 13.1 %collective-permute-start.11 = (bf16[128,768]{1,0:T(8,128)(2,1)S(1)}, bf16[128,768]{1,0:T(8,128)(2,1)S(1)}, u32[]{:S(2)}, u32[]{:S(2)}) collective-permute-start(bf16[128,768]{1,0:T(8,128)(2,1)S(1)} %get-tuple-element.7), channel_id=1, source_target_pairs={{0,2},{1,3},{2,4},{3,5},{4,6},{5,7},{6,0},{7,1},{8,14},{9,15},{10,... | collective-permute-start | bytes 589832 | tf_op jit(solution)/shard_map/ppermute | solution.py:40
  70.4 17.0 %collective-permute-start.10 = (bf16[2,128,768]{2,1,0:T(8,128)(2,1)S(1)}, bf16[2,128,768]{2,1,0:T(8,128)(2,1)S(1)}, u32[]{:S(2)}, u32[]{:S(2)}) collective-permute-start(bf16[2,128,768]{2,1,0:T(8,128)(2,1)S(1)} %pad_maximum_fusion.1), channel_id=1, source_target_pairs={{0,7},{1,0},{2,1},{3,2},{4,3},{5,4},{6,5},{7,6},{8,9},{9,10},{10,1... | collective-permute-start | bytes 1179656 | tf_op jit(solution)/shard_map/ppermute | solution.py:40
  83.3 8.6 %collective-permute-start.12 = (bf16[128,768]{1,0:T(8,128)(2,1)S(1)}, bf16[128,768]{1,0:T(8,128)(2,1)S(1)}, u32[]{:S(2)}, u32[]{:S(2)}) collective-permute-start(bf16[128,768]{1,0:T(8,128)(2,1)S(1)} %fusion.10), channel_id=1, source_target_pairs={{0,2},{1,3},{2,4},{3,5},{4,6},{5,7},{6,0},{7,1},{8,14},{9,15},{10,... | collective-permute-start | bytes 589832 | tf_op jit(solution)/shard_map/ppermute | solution.py:40
  88.5 9.2 %collective-permute-start.13 = (bf16[128,768]{1,0:T(8,128)(2,1)S(1)}, bf16[128,768]{1,0:T(8,128)(2,1)S(1)}, u32[]{:S(2)}, u32[]{:S(2)}) collective-permute-start(bf16[128,768]{1,0:T(8,128)(2,1)S(1)} %fusion.18), channel_id=1, source_target_pairs={{0,6},{1,7},{2,0},{3,1},{4,2},{5,3},{6,4},{7,5},{8,10},{9,11},{10,... | collective-permute-start | bytes 589832 | tf_op jit(solution)/shard_map/ppermute | solution.py:40
  103.8 24.1 %copy-start.3 = (f32[8192]{0:T(1024)S(1)}, f32[8192]{0:T(1024)}, u32[]{:S(2)}) copy-start(f32[8192]{0:T(1024)} %param.7) | copy-start | bytes 98308
  103.9 5.9 %collective-permute-start.15 = (bf16[2,128,256]{2,1,0:T(8,128)(2,1)S(1)}, bf16[2,128,256]{2,1,0:T(8,128)(2,1)S(1)}, u32[]{:S(2)}, u32[]{:S(2)}) collective-permute-start(bf16[2,128,256]{2,1,0:T(8,128)(2,1)S(1)} %pad_maximum_fusion.2), channel_id=1, source_target_pairs={{0,7},{1,0},{2,1},{3,2},{4,3},{5,4},{6,5},{7,6},{8,9},{9,10},{10,1... | collective-permute-start | bytes 393224 | tf_op jit(solution)/shard_map/ppermute | solution.py:40
  104.0 5.9 %collective-permute-start.17 = (bf16[128,256]{1,0:T(8,128)(2,1)S(1)}, bf16[128,256]{1,0:T(8,128)(2,1)S(1)}, u32[]{:S(2)}, u32[]{:S(2)}) collective-permute-start(bf16[128,256]{1,0:T(8,128)(2,1)S(1)} %get-tuple-element.12), channel_id=1, source_target_pairs={{0,6},{1,7},{2,0},{3,1},{4,2},{5,3},{6,4},{7,5},{8,10},{9,11},{10,... | collective-permute-start | bytes 196616 | tf_op jit(solution)/shard_map/ppermute | solution.py:40
  104.1 6.0 %collective-permute-start.16 = (bf16[2,128,256]{2,1,0:T(8,128)(2,1)S(1)}, bf16[2,128,256]{2,1,0:T(8,128)(2,1)S(1)}, u32[]{:S(2)}, u32[]{:S(2)}) collective-permute-start(bf16[2,128,256]{2,1,0:T(8,128)(2,1)S(1)} %pad_maximum_fusion.3), channel_id=1, source_target_pairs={{0,1},{1,2},{2,3},{3,4},{4,5},{5,6},{6,7},{7,0},{8,15},{9,8},{10,9... | collective-permute-start | bytes 393224 | tf_op jit(solution)/shard_map/ppermute | solution.py:40
  109.9 5.9 %collective-permute-start.18 = (bf16[128,256]{1,0:T(8,128)(2,1)S(1)}, bf16[128,256]{1,0:T(8,128)(2,1)S(1)}, u32[]{:S(2)}, u32[]{:S(2)}) collective-permute-start(bf16[128,256]{1,0:T(8,128)(2,1)S(1)} %fusion.24), channel_id=1, source_target_pairs={{0,6},{1,7},{2,0},{3,1},{4,2},{5,3},{6,4},{7,5},{8,10},{9,11},{10,... | collective-permute-start | bytes 196616 | tf_op jit(solution)/shard_map/ppermute | solution.py:40
  110.1 5.7 %collective-permute-start.19 = (bf16[128,256]{1,0:T(8,128)(2,1)S(1)}, bf16[128,256]{1,0:T(8,128)(2,1)S(1)}, u32[]{:S(2)}, u32[]{:S(2)}) collective-permute-start(bf16[128,256]{1,0:T(8,128)(2,1)S(1)} %fusion.32), channel_id=1, source_target_pairs={{0,2},{1,3},{2,4},{3,5},{4,6},{5,7},{6,0},{7,1},{8,14},{9,15},{10,... | collective-permute-start | bytes 196616 | tf_op jit(solution)/shard_map/ppermute | solution.py:40
  117.8 24.3 %all-to-all-start = ((bf16[32,3,4,1024]{3,2,1,0:T(4,128)(2,1)}), bf16[32,3,4,1024]{3,2,1,0:T(4,128)(2,1)S(1)}, u32[]{:S(2)}, u32[]{:S(2)}) async-start(bf16[32,3,4,1024]{3,2,1,0:T(4,128)(2,1)} %copy.14), calls=%async_computation | async-start | bytes 1572864 | tf_op jit(solution)/shard_map/all_to_all | solution.py:130
